TPU v7x, 256 devices: a whole 4x4x8 slice. The times are simulated.
256 devices in a mesh: epoch: 8 (over x, y_lo), sky: 32 (over z, y_hi, core).
Axes of the slice: x: 4, y: 4 (y_hi: 2, y_lo: 2; y = y_hi * 2 + y_lo), z: 8, core: 2. Of those that a mesh axis runs over, the one named last changes fastest.
Arguments:
- image: bfloat16 [16, 1536, 2048], P('epoch', 'sky'), may hold values from -400 to 400
- inv_variance: bfloat16 [16, 1536, 2048], P('epoch', 'sky'), may hold values from 0.25 to 4
- psf_rows: float32 [9], replicated, may hold values from 0.05 to 1
- psf_cols: float32 [9], replicated, may hold values from 0.05 to 1
- shift_num: int32 [4, 16], replicated, may hold values from -64 to 64, as said below
Outputs:
- search_map: float32 [1536, 2048], P('sky', 'epoch')
Inputs may be any that keep to these rules, and one draw needn't show every extreme that they name: `shift_num`: at level l every entry has magnitude at most 4 * 2 * 2^l, and at each level some entry equals plus and some other entry minus that bound.
All inputs are finite; a program needn't handle non-finite values.
Results may differ from a plain program's by a relative error of at most 0.0024.
Values may be sent and summed in bfloat16 or wider, within the bound.
No kernel may reach another device: no remote copies, remote signals or barrier semaphores. Data moves between devices by JAX's collectives and lax.ppermute only.
A program may use at most 64 MiB of HBM per device.

v0:
```python
import jax
import jax.numpy as jnp
from jax import lax
from jax.sharding import PartitionSpec as P

LEVELS = 4
PSF_HALF = 4
DEN = 4
VMAX = 2


def padded_2(x, sides, width):
    for axis, dim in sides:
        size, length = (lax.axis_size(axis), x.shape[dim])
        up = [(i, (i + 1) % size) for i in range(size - 1)]
        down = [(j, i) for i, j in up]
        last = lax.slice_in_dim(x, length - width, length, axis=dim)
        leading = lax.slice_in_dim(x, 0, width, axis=dim)
        before = lax.ppermute(last, axis, up)
        after = lax.ppermute(leading, axis, down)
        x = jnp.concatenate([before, x, after], axis=dim)
    return x


def from_partner(block, axis, distance):
    count = lax.axis_size(axis)
    route = []
    for low in range(count):
        high = low | 1 << distance
        if high != low and high < count:
            route += [(low, high), (high, low)]
    return lax.ppermute(block, axis, route)


def combined_all(x, axis, combine):
    everything = jax.tree.map(lambda part: lax.all_gather(part, axis), x)
    leading = jax.tree.map(lambda part: part[0], everything)

    def step(k, so_far):
        return combine(so_far, jax.tree.map(lambda part: part[k], everything))

    return lax.fori_loop(1, lax.axis_size(axis), step, leading)


def shift_rows(padded, numerators, rim_width):
    row_count = padded.shape[2] - 2 * rim_width
    whole_rows = jnp.floor_divide(numerators, DEN)
    fraction = (numerators - whole_rows * DEN).astype(jnp.float32) / DEN
    start_rows = rim_width - whole_rows - 1

    def take_rows(one_block, start):
        return lax.dynamic_slice_in_dim(one_block, start, row_count + 1, axis=1)

    taken_rows = jax.vmap(take_rows)(padded, start_rows)
    fraction = fraction[:, None, None, None]
    return (1.0 - fraction) * taken_rows[:, :, 1:] + fraction * taken_rows[:, :, :-1]


def rim_shift(upper_half, numerators, rim_width):
    padded = padded_2(upper_half, (("sky", 2),), rim_width)
    return [shift_rows(padded, numbers, rim_width) for numbers in numerators]


def local_level(stacks, numerators, level_index):
    count = stacks.shape[0]
    row_count = stacks.shape[2]
    col_count = stacks.shape[3]
    half_span = 2**level_index
    groups = count // (2 * half_span)
    rim_width = VMAX * half_span + 1
    paired = stacks.reshape(groups, 2, half_span, 2, row_count, col_count)
    lower_half = paired[:, 0].reshape(groups * half_span, 2, row_count, col_count)
    upper_half = paired[:, 1].reshape(groups * half_span, 2, row_count, col_count)
    numbers = numerators.reshape(groups, 2, half_span)
    moved = rim_shift(upper_half, (numbers[:, 0].reshape(-1), numbers[:, 1].reshape(-1)), rim_width)
    new_lower = lower_half + moved[0]
    new_upper = lower_half + moved[1]
    stacks = jnp.stack(
        [
            new_lower.reshape(groups, half_span, 2, row_count, col_count),
            new_upper.reshape(groups, half_span, 2, row_count, col_count),
        ],
        axis=1,
    )
    return stacks.reshape(count, 2, row_count, col_count)


def filter_maps(padded_in, psf_rows, psf_cols):
    reach = PSF_HALF
    variance = padded_in[1].astype(jnp.float32)
    weighted = padded_in[0].astype(jnp.float32) * variance
    ep_count = padded_in.shape[1]
    out_rows = padded_in.shape[2] - 2 * reach
    width = padded_in.shape[3]
    rows_psi = jnp.zeros((ep_count, out_rows, width), jnp.float32)
    rows_phi = jnp.zeros((ep_count, out_rows, width), jnp.float32)
    for offset in range(2 * reach + 1):
        rows_psi = rows_psi + psf_rows[offset] * weighted[:, offset : offset + out_rows, :]
        rows_phi = (
            rows_phi
            + psf_rows[offset] * psf_rows[offset] * variance[:, offset : offset + out_rows, :]
        )
    rows_psi = jnp.pad(rows_psi, ((0, 0), (0, 0), (reach, reach)))
    rows_phi = jnp.pad(rows_phi, ((0, 0), (0, 0), (reach, reach)))
    psi_map = jnp.zeros((ep_count, out_rows, width), jnp.float32)
    phi_map = jnp.zeros((ep_count, out_rows, width), jnp.float32)
    for offset in range(2 * reach + 1):
        psi_map = psi_map + psf_cols[offset] * rows_psi[:, :, offset : offset + width]
        phi_map = (
            phi_map + psf_cols[offset] * psf_cols[offset] * rows_phi[:, :, offset : offset + width]
        )
    return jnp.stack([psi_map, phi_map], axis=1)


def combine_pairs(first, second):
    top_value = jnp.maximum(first[0], second[0])
    total = first[1] * jnp.exp(first[0] - top_value) + second[1] * jnp.exp(second[0] - top_value)
    return (top_value, total)


def on_device(image, inv_variance, psf_rows, psf_cols, shift_num):
    ep_count = image.shape[0]
    col_count = image.shape[2]
    epoch_count = lax.axis_size("epoch")
    my_epoch = lax.axis_index("epoch")
    inputs = jnp.stack([image, inv_variance])
    padded_in = padded_2(inputs, (("sky", 2),), PSF_HALF)
    block_cols = col_count // epoch_count
    stacks = filter_maps(padded_in, psf_rows, psf_cols)
    local_levels = ep_count.bit_length() - 1
    for level_index in range(LEVELS):
        mine = lax.dynamic_slice_in_dim(shift_num[level_index], my_epoch * ep_count, ep_count)
        if level_index < local_levels:
            stacks = local_level(stacks, mine, level_index)
        else:
            bit_number = level_index - local_levels
            partner = from_partner(stacks, "epoch", bit_number)
            is_lower = my_epoch >> bit_number & 1 == 0
            lower_half = jnp.where(is_lower, stacks, partner)
            upper_half = jnp.where(is_lower, partner, stacks)
            rim_width = VMAX * 2**level_index + 1
            stacks = lower_half + rim_shift(upper_half, (mine,), rim_width)[0]
    likelihood = stacks[:, 0] / jnp.sqrt(stacks[:, 1])
    local_peak = jnp.max(likelihood, axis=0)
    local_total = jnp.sum(jnp.exp(likelihood - local_peak[None]), axis=0)
    peak_value, total = combined_all((local_peak, local_total), "epoch", combine_pairs)
    peak_value = lax.dynamic_slice_in_dim(peak_value, my_epoch * block_cols, block_cols, 1)
    total = lax.dynamic_slice_in_dim(total, my_epoch * block_cols, block_cols, 1)
    return peak_value + jnp.log(total)


def solution(mesh):
    return jax.shard_map(
        on_device,
        mesh=mesh,
        in_specs=(P("epoch", "sky", None), P("epoch", "sky", None), P(), P(), P()),
        out_specs=P("sky", "epoch"),
        check_vma=False,
    )
```

profile of v0, /device:TPU:129, one launch (start us, length us, event | category | flops | bytes accessed | tf_op | source)
XLA Modules:
  0.0 442.6 jit_solution(17566693236650760590)
XLA Ops:
  7.5 5.4 %collective-permute-start = (bf16[2,2,4,2048]{3,2,1,0:T(4,128)(2,1)S(1)}, bf16[2,2,4,2048]{3,2,1,0:T(4,128)(2,1)S(1)}, u32[]{:S(2)}, u32[]{:S(2)}) collective-permute-start(bf16[2,2,4,2048]{3,2,1,0:T(4,128)(2,1)S(1)} %get-tuple-element.192), channel_id=1, source_target_pairs={{0,1},{1,2},{2,3},{3,4},{4,5},{5,6},{6,7},{7,8},{8,9},{9,10},{10,1... | collective-permute-start | bytes 196616 | tf_op jit(solution)/shard_map/ppermute | solution.py:19
  12.9 1.9 collective-permute-start.1
  14.9 1.7 fusion.66
  16.5 1.7 fusion.65
  43.0 6.4 %fusion.23 = f32[2,48,2048]{2,1,0:T(8,128)S(1)} fusion(f32[2,56,2048]{2,1,0:T(8,128)S(1)} %convert_multiply_fusion, f32[]{:T(128)} %bitcast.15, f32[]{:T(128)} %bitcast.14, f32[]{:T(128)} %bitcast.13, f32[]{:T(128)} %bitcast.12, f32[]{:T(128)} %bitcast.11, f32[]{:T(128)} %bitcast.10, f32[]{:T(128)} %bitcast.9, f32[]{:T(128)} %bitcast.8, f32[]{:T(128)} %bitcast.3), kind=kLoop, calls=%fused_computation.63 | loop fusion | flops 3342336 | bytes 7864356 | tf_op jit(solution)/shard_map/add | solution.py:98
  49.4 7.2 %add_bitcast_fusion = f32[2,1,48,2048]{3,2,0,1:T(8,128)S(1)} fusion(f32[2,48,2048]{2,1,0:T(8,128)S(1)} %fusion.23, f32[]{:T(128)} %bitcast.23, f32[]{:T(128)} %bitcast.22, f32[]{:T(128)} %bitcast.21, f32[]{:T(128)} %bitcast.20, f32[]{:T(128)} %bitcast.19, f32[]{:T(128)} %bitcast.18, f32[]{:T(128)} %bitcast.17, f32[]{:T(128)} %bitcast.16, f32[]{:T(128)} %bitcast.2), kind=kLoop, calls=%fused_computation.91 | loop fusion | flops 3342336 | bytes 1572900 | tf_op jit(solution)/shard_map/stack | solution.py:112
  58.3 1.7 multiply_add_fusion
  60.5 1.4 maximum_bitcast_fusion
  62.0 5.1 %collective-permute-start.2 = (f32[1,2,3,2048]{3,1,2,0:T(2,128)S(1)}, f32[1,2,3,2048]{3,1,2,0:T(2,128)S(1)}, u32[]{:S(2)}, u32[]{:S(2)}) collective-permute-start(f32[1,2,3,2048]{3,1,2,0:T(2,128)S(1)} %get-tuple-element.190), channel_id=1, source_target_pairs={{0,1},{1,2},{2,3},{3,4},{4,5},{5,6},{6,7},{7,8},{8,9},{9,10},{10,1... | collective-permute-start | bytes 147464 | tf_op jit(solution)/shard_map/ppermute | solution.py:19
  67.2 2.1 collective-permute-start.3
  76.5 1.9 fusion.14
  78.4 2.0 maximum_bitcast_fusion.1
  81.0 30.8 %collective-permute-done.4 = f32[2,2,48,2048]{3,1,2,0:T(2,128)S(1)} collective-permute-done((f32[2,2,48,2048]{3,1,2,0:T(2,128)}, f32[2,2,48,2048]{3,1,2,0:T(2,128)S(1)}, u32[]{:S(2)}, u32[]{:S(2)}) %collective-permute-start.4) | collective-permute-done | bytes 1572896 | tf_op jit(solution)/shard_map/ppermute | solution.py:32
  111.8 1.5 broadcast_select_fusion
  113.4 9.2 %collective-permute-start.5 = (f32[2,2,5,2048]{3,1,2,0:T(2,128)S(1)}, f32[2,2,5,2048]{3,1,2,0:T(2,128)S(1)}, u32[]{:S(2)}, u32[]{:S(2)}) collective-permute-start(f32[2,2,5,2048]{3,1,2,0:T(2,128)S(1)} %get-tuple-element.188), channel_id=1, source_target_pairs={{0,1},{1,2},{2,3},{3,4},{4,5},{5,6},{6,7},{7,8},{8,9},{9,10},{10,1... | collective-permute-start | bytes 491528 | tf_op jit(solution)/shard_map/ppermute | solution.py:19
  122.6 1.9 collective-permute-start.6
  124.9 5.9 %collective-permute-done.6 = f32[2,2,5,2048]{3,1,2,0:T(2,128)S(1)} collective-permute-done((f32[2,2,5,2048]{3,1,2,0:T(2,128)S(1)}, f32[2,2,5,2048]{3,1,2,0:T(2,128)S(1)}, u32[]{:S(2)}, u32[]{:S(2)}) %collective-permute-start.6) | collective-permute-done | bytes 163872 | tf_op jit(solution)/shard_map/ppermute | solution.py:20
  131.8 1.5 copy.8
  133.2 3.8 gather_fusion
  137.0 2.9 fusion.7
  141.3 34.6 %collective-permute-done.7 = f32[2,2,48,2048]{3,1,2,0:T(2,128)S(1)} collective-permute-done((f32[2,2,48,2048]{3,1,2,0:T(2,128)S(1)}, f32[2,2,48,2048]{3,1,2,0:T(2,128)S(1)}, u32[]{:S(2)}, u32[]{:S(2)}) %collective-permute-start.7) | collective-permute-done | bytes 1572896 | tf_op jit(solution)/shard_map/ppermute | solution.py:32
  177.0 1.9 collective-permute-start.8
  179.0 3.1 collective-permute-start.9
  182.6 9.1 %collective-permute-done.9 = f32[2,2,9,2048]{3,1,2,0:T(2,128)S(1)} collective-permute-done((f32[2,2,9,2048]{3,1,2,0:T(2,128)S(1)}, f32[2,2,9,2048]{3,1,2,0:T(2,128)S(1)}, u32[]{:S(2)}, u32[]{:S(2)}) %collective-permute-start.9) | collective-permute-done | bytes 294944 | tf_op jit(solution)/shard_map/ppermute | solution.py:20
  192.8 2.6 copy.9
  195.4 3.9 gather_fusion.1
  199.3 2.9 fusion.5
  202.2 2.8 collective-permute-start.10
  205.0 34.9 %collective-permute-done.10 = f32[2,2,48,2048]{3,1,2,0:T(2,128)S(1)} collective-permute-done((f32[2,2,48,2048]{3,1,2,0:T(2,128)S(1)}, f32[2,2,48,2048]{3,1,2,0:T(2,128)S(1)}, u32[]{:S(2)}, u32[]{:S(2)}) %collective-permute-start.10) | collective-permute-done | bytes 1572896 | tf_op jit(solution)/shard_map/ppermute | solution.py:32
  241.2 2.3 collective-permute-start.11
  243.5 2.2 collective-permute-start.12
  245.8 10.0 %collective-permute-done.11 = f32[2,2,17,2048]{3,1,2,0:T(2,128)S(1)} collective-permute-done((f32[2,2,17,2048]{3,1,2,0:T(2,128)S(1)}, f32[2,2,17,2048]{3,1,2,0:T(2,128)S(1)}, u32[]{:S(2)}, u32[]{:S(2)}) %collective-permute-start.11) | collective-permute-done | bytes 557088 | tf_op jit(solution)/shard_map/ppermute | solution.py:19
  255.9 5.7 %collective-permute-done.12 = f32[2,2,17,2048]{3,1,2,0:T(2,128)S(1)} collective-permute-done((f32[2,2,17,2048]{3,1,2,0:T(2,128)S(1)}, f32[2,2,17,2048]{3,1,2,0:T(2,128)S(1)}, u32[]{:S(2)}, u32[]{:S(2)}) %collective-permute-start.12) | collective-permute-done | bytes 557088 | tf_op jit(solution)/shard_map/ppermute | solution.py:20
  261.6 1.5 pad_maximum_fusion
  263.1 2.6 copy.10
  265.7 4.0 gather_fusion.2
  269.8 2.2 fusion.3
  271.9 2.0 fusion.54
  275.9 72.3 %all-gather.7.cloned.1.call-done = f32[384,2048]{1,0:T(8,128)} async-done(((f32[48,2048]{1,0:T(8,128)}), f32[384,2048]{1,0:T(8,128)}) %all-gather.7.cloned.1.call-update) | async-done | bytes 3145744 | tf_op jit(solution)/shard_map/all_gather | solution.py:36
  349.2 74.5 %all-gather.5.cloned.1.call-done = f32[384,2048]{1,0:T(8,128)} async-done(((f32[48,2048]{1,0:T(8,128)}), f32[384,2048]{1,0:T(8,128)}) %all-gather.5.cloned.1.call-update) | async-done | bytes 3145744 | tf_op jit(solution)/shard_map/all_gather | solution.py:36
  424.8 10.4 %while.19 = (s32[]{:T(128)}, f32[48,2048]{1,0:T(8,128)S(1)}, f32[48,2048]{1,0:T(8,128)S(1)}, f32[8,48,2048]{2,1,0:T(8,128)}, f32[8,48,2048]{2,1,0:T(8,128)}, /*index=5*/s32[]{:T(128)}, s32[]{:T(128)}, s32[]{:T(128)}) while((s32[]{:T(128)}, f32[48,2048]{1,0:T(8,128)S(1)}, f32[48,2048]{1,0:T(8,128)S(1)}, f32[8,48,2048]{2,1,0:T(8,128)}, ...), condition=%wide.region_3.4_spmd, body=%wide.region_2.3_spmd.sunk | while | flops 589829 | bytes 2359427 | solution.py:42
  424.8 1.5 fusion.68
  426.3 1.5 fusion.68
  427.8 1.5 fusion.68
  429.2 1.5 fusion.68
  430.7 1.5 fusion.68
  432.2 1.5 fusion.68
  433.7 1.5 fusion.68
  (56 shorter events, 18.8 us)
Async XLA Ops:
  6.5 341.7 %all-gather.7.cloned.1.call-start = ((), (), s32[]{:S(2)}) async-start(), calls=%async_computation.1 | async-start | bytes 3538944 | tf_op jit(solution)/shard_map/all_gather | solution.py:36
  7.5 33.9 %collective-permute-start = (bf16[2,2,4,2048]{3,2,1,0:T(4,128)(2,1)S(1)}, bf16[2,2,4,2048]{3,2,1,0:T(4,128)(2,1)S(1)}, u32[]{:S(2)}, u32[]{:S(2)}) collective-permute-start(bf16[2,2,4,2048]{3,2,1,0:T(4,128)(2,1)S(1)} %get-tuple-element.192), channel_id=1, source_target_pairs={{0,1},{1,2},{2,3},{3,4},{4,5},{5,6},{6,7},{7,8},{8,9},{9,10},{10,1... | collective-permute-start | bytes 196616 | tf_op jit(solution)/shard_map/ppermute | solution.py:19
  12.9 28.5 %collective-permute-start.1 = (bf16[2,2,4,2048]{3,2,1,0:T(4,128)(2,1)S(1)}, bf16[2,2,4,2048]{3,2,1,0:T(4,128)(2,1)S(1)}, u32[]{:S(2)}, u32[]{:S(2)}) collective-permute-start(bf16[2,2,4,2048]{3,2,1,0:T(4,128)(2,1)S(1)} %get-tuple-element.193), channel_id=1, source_target_pairs={{1,0},{2,1},{3,2},{4,3},{5,4},{6,5},{7,6},{8,7},{9,8},{10,9},{11,1... | collective-permute-start | bytes 196616 | tf_op jit(solution)/shard_map/ppermute | solution.py:20
  62.0 14.0 %collective-permute-start.2 = (f32[1,2,3,2048]{3,1,2,0:T(2,128)S(1)}, f32[1,2,3,2048]{3,1,2,0:T(2,128)S(1)}, u32[]{:S(2)}, u32[]{:S(2)}) collective-permute-start(f32[1,2,3,2048]{3,1,2,0:T(2,128)S(1)} %get-tuple-element.190), channel_id=1, source_target_pairs={{0,1},{1,2},{2,3},{3,4},{4,5},{5,6},{6,7},{7,8},{8,9},{9,10},{10,1... | collective-permute-start | bytes 147464 | tf_op jit(solution)/shard_map/ppermute | solution.py:19
  67.2 8.8 %collective-permute-start.3 = (f32[1,2,3,2048]{3,1,2,0:T(2,128)S(1)}, f32[1,2,3,2048]{3,1,2,0:T(2,128)S(1)}, u32[]{:S(2)}, u32[]{:S(2)}) collective-permute-start(f32[1,2,3,2048]{3,1,2,0:T(2,128)S(1)} %get-tuple-element.191), channel_id=1, source_target_pairs={{1,0},{2,1},{3,2},{4,3},{5,4},{6,5},{7,6},{8,7},{9,8},{10,9},{11,1... | collective-permute-start | bytes 147464 | tf_op jit(solution)/shard_map/ppermute | solution.py:20
  78.4 33.5 %copy-start.1 = (f32[1,1,1,2,48,2048]{5,3,4,1,2,0:T(2,128)}, f32[1,1,1,2,48,2048]{5,3,4,1,2,0:T(2,128)S(1)}, u32[]{:S(2)}) copy-start(f32[1,1,1,2,48,2048]{5,3,4,1,2,0:T(2,128)S(1)} %get-tuple-element.182) | copy-start | bytes 2359300
  78.4 33.5 %copy-start.2 = (f32[1,1,1,2,48,2048]{5,3,4,1,2,0:T(2,128)}, f32[1,1,1,2,48,2048]{5,3,4,1,2,0:T(2,128)S(1)}, u32[]{:S(2)}) copy-start(f32[1,1,1,2,48,2048]{5,3,4,1,2,0:T(2,128)S(1)} %get-tuple-element.183) | copy-start | bytes 2359300
  80.4 31.4 %collective-permute-start.4 = (f32[2,2,48,2048]{3,1,2,0:T(2,128)}, f32[2,2,48,2048]{3,1,2,0:T(2,128)S(1)}, u32[]{:S(2)}, u32[]{:S(2)}) collective-permute-start(f32[2,2,48,2048]{3,1,2,0:T(2,128)} %maximum_bitcast_fusion.1), channel_id=1, source_target_pairs={{0,32},{32,0},{64,96},{96,64},{128,160},{160,128},{192,224},{224,1... | collective-permute-start | bytes 4718600 | tf_op jit(solution)/shard_map/ppermute | solution.py:32
  111.8 1.5 copy-start.4
  113.4 11.5 %collective-permute-start.5 = (f32[2,2,5,2048]{3,1,2,0:T(2,128)S(1)}, f32[2,2,5,2048]{3,1,2,0:T(2,128)S(1)}, u32[]{:S(2)}, u32[]{:S(2)}) collective-permute-start(f32[2,2,5,2048]{3,1,2,0:T(2,128)S(1)} %get-tuple-element.188), channel_id=1, source_target_pairs={{0,1},{1,2},{2,3},{3,4},{4,5},{5,6},{6,7},{7,8},{8,9},{9,10},{10,1... | collective-permute-start | bytes 491528 | tf_op jit(solution)/shard_map/ppermute | solution.py:19
  122.6 8.1 %collective-permute-start.6 = (f32[2,2,5,2048]{3,1,2,0:T(2,128)S(1)}, f32[2,2,5,2048]{3,1,2,0:T(2,128)S(1)}, u32[]{:S(2)}, u32[]{:S(2)}) collective-permute-start(f32[2,2,5,2048]{3,1,2,0:T(2,128)S(1)} %get-tuple-element.189), channel_id=1, source_target_pairs={{1,0},{2,1},{3,2},{4,3},{5,4},{6,5},{7,6},{8,7},{9,8},{10,9},{11,1... | collective-permute-start | bytes 491528 | tf_op jit(solution)/shard_map/ppermute | solution.py:20
  139.9 36.1 %copy-start = (f32[2,2,48,2048]{3,1,2,0:T(2,128)}, f32[2,2,48,2048]{3,1,2,0:T(2,128)S(1)}, u32[]{:S(2)}) copy-start(f32[2,2,48,2048]{3,1,2,0:T(2,128)S(1)} %fusion.7) | copy-start | bytes 4718596
  140.0 35.9 %collective-permute-start.7 = (f32[2,2,48,2048]{3,1,2,0:T(2,128)S(1)}, f32[2,2,48,2048]{3,1,2,0:T(2,128)S(1)}, u32[]{:S(2)}, u32[]{:S(2)}) collective-permute-start(f32[2,2,48,2048]{3,1,2,0:T(2,128)S(1)} %fusion.7), channel_id=1, source_target_pairs={{0,64},{64,0},{32,96},{96,32},{128,192},{192,128},{160,224},{224,1... | collective-permute-start | bytes 4718600 | tf_op jit(solution)/shard_map/ppermute | solution.py:32
  175.8 1.2 copy-start.5
  177.0 5.6 %collective-permute-start.8 = (f32[2,2,9,2048]{3,1,2,0:T(2,128)S(1)}, f32[2,2,9,2048]{3,1,2,0:T(2,128)S(1)}, u32[]{:S(2)}, u32[]{:S(2)}) collective-permute-start(f32[2,2,9,2048]{3,1,2,0:T(2,128)S(1)} %get-tuple-element.186), channel_id=1, source_target_pairs={{0,1},{1,2},{2,3},{3,4},{4,5},{5,6},{6,7},{7,8},{8,9},{9,10},{10,1... | collective-permute-start | bytes 884744 | tf_op jit(solution)/shard_map/ppermute | solution.py:19
  179.0 12.7 %collective-permute-start.9 = (f32[2,2,9,2048]{3,1,2,0:T(2,128)S(1)}, f32[2,2,9,2048]{3,1,2,0:T(2,128)S(1)}, u32[]{:S(2)}, u32[]{:S(2)}) collective-permute-start(f32[2,2,9,2048]{3,1,2,0:T(2,128)S(1)} %get-tuple-element.187), channel_id=1, source_target_pairs={{1,0},{2,1},{3,2},{4,3},{5,4},{6,5},{7,6},{8,7},{9,8},{10,9},{11,1... | collective-permute-start | bytes 884744 | tf_op jit(solution)/shard_map/ppermute | solution.py:20
  202.2 37.7 %collective-permute-start.10 = (f32[2,2,48,2048]{3,1,2,0:T(2,128)S(1)}, f32[2,2,48,2048]{3,1,2,0:T(2,128)S(1)}, u32[]{:S(2)}, u32[]{:S(2)}) collective-permute-start(f32[2,2,48,2048]{3,1,2,0:T(2,128)S(1)} %fusion.5), channel_id=1, source_target_pairs={{0,128},{128,0},{32,160},{160,32},{64,192},{192,64},{96,224},{224,... | collective-permute-start | bytes 4718600 | tf_op jit(solution)/shard_map/ppermute | solution.py:32
  239.9 1.2 copy-start.3
  241.2 14.7 %collective-permute-start.11 = (f32[2,2,17,2048]{3,1,2,0:T(2,128)S(1)}, f32[2,2,17,2048]{3,1,2,0:T(2,128)S(1)}, u32[]{:S(2)}, u32[]{:S(2)}) collective-permute-start(f32[2,2,17,2048]{3,1,2,0:T(2,128)S(1)} %get-tuple-element.184), channel_id=1, source_target_pairs={{0,1},{1,2},{2,3},{3,4},{4,5},{5,6},{6,7},{7,8},{8,9},{9,10},{10,1... | collective-permute-start | bytes 1671176 | tf_op jit(solution)/shard_map/ppermute | solution.py:19
  243.5 18.1 %collective-permute-start.12 = (f32[2,2,17,2048]{3,1,2,0:T(2,128)S(1)}, f32[2,2,17,2048]{3,1,2,0:T(2,128)S(1)}, u32[]{:S(2)}, u32[]{:S(2)}) collective-permute-start(f32[2,2,17,2048]{3,1,2,0:T(2,128)S(1)} %get-tuple-element.185), channel_id=1, source_target_pairs={{1,0},{2,1},{3,2},{4,3},{5,4},{6,5},{7,6},{8,7},{9,8},{10,9},{11,1... | collective-permute-start | bytes 1671176 | tf_op jit(solution)/shard_map/ppermute | solution.py:20
  274.0 1.2 copy-start.6
  275.2 148.6 %all-gather.5.cloned.1.call-start = ((), (), s32[]{:S(2)}) async-start(), calls=%async_computation | async-start | bytes 3538944 | tf_op jit(solution)/shard_map/all_gather | solution.py:36
Sparse Core Ops, SparseCore 0:
  275.3 72.8 all-gather.6
  350.0 73.7 all-gather.4
where the time goes:
time: 447 us; the launch traced here: 443 us
  waiting for transfers between devices  279 us (62%)
  other arithmetic  52.5 us (12%)
  between operations  42.2 us (9%)
  starting transfers between devices  40 us (9%)
  local copies, waits for them, and re-layouts  28.8 us (6%)
    all_gather x2, waiting for transfers between devices, combined_all(): everything = jax.tree.map(lambda part: lax.all_gather(part, axis), x)  147 us
    ppermute x3, waiting for transfers between devices, from_partner(): return lax.ppermute(block, axis, route)  100 us
    ppermute x5, starting transfers between devices, padded_2(): before = lax.ppermute(last, axis, up)  23.9 us
    ppermute x5, waiting for transfers between devices, padded_2(): after = lax.ppermute(leading, axis, down)  20.7 us
    gather x3, local copies, waits for them, and re-layouts, take_rows(): return lax.dynamic_slice_in_dim(one_block, start, row_count + 1, axis=1)  11.7 us
    ppermute x5, starting transfers between devices, padded_2(): after = lax.ppermute(leading, axis, down)  11.3 us
    ppermute x5, waiting for transfers between devices, padded_2(): before = lax.ppermute(last, axis, up)  10.5 us
    add x7, other arithmetic, combine_pairs(): first[1] * jnp.exp(first[0] - top_value)  10.2 us
  transfers between devices with their start and end apart: 15, of which 11 were waited for; matrix products, arithmetic and copies ran while one was open for 1% of the time, Pallas kernels for 0%

commit v1 on v0

v1 whole, which is shorter than its diff:
```python
import jax
import jax.numpy as jnp
from jax import lax
from jax.experimental import pallas as pl
from jax.experimental.pallas import tpu as pltpu
from jax.sharding import PartitionSpec as P

EPOCHS = 16
LEVELS = 4
PSF = 9
REACH = 4
PEERS = 8
ROWS = 48
LANES = 128
COLS = 256
EDGE_ROW = 8 * ROWS
SEND_ROWS = 9 * ROWS
HALO = [2 * j + REACH for j in range(EPOCHS)]
HALO_AT = [sum(HALO[:j]) for j in range(EPOCHS)]
HALO_ROWS = sum(HALO)
EDGE_LO = HALO[7]
EDGE_HI = HALO[15]
EDGE_LO_AT = 4 * HALO_ROWS
EDGE_HI_AT = EDGE_LO_AT + EDGE_LO
HALO_SEND = 1280
BASE = 40
SPAN = 128
F32 = jnp.float32
BF16 = jnp.bfloat16


def edge_lane(array, j):
    return 32 * ((j // 2) % 4) + (2 * array + j % 2) * 8


def pack_kernel(where_ref, image_ref, variance_ref, out_ref):
    turn = 32 * (where_ref[0] % 4)
    lane = lax.broadcasted_iota(jnp.int32, (ROWS, LANES), 1)
    for c in range(PEERS):
        edges = jnp.zeros((ROWS, LANES), F32)
        for a, ref in enumerate((image_ref, variance_ref)):
            for i in range(2):
                for t in range(2):
                    row = ((a * 2 + i) * 2 + t) * ROWS
                    out_ref[c, row : row + ROWS, :] = ref[i, :, (2 * c + t) * LANES : (2 * c + t + 1) * LANES]
                picked = jnp.zeros((ROWS, LANES), F32)
                if c > 0:
                    left = ref[i, :, (2 * c - 1) * LANES : 2 * c * LANES].astype(F32)
                    picked = jnp.where(lane >= LANES - REACH, left, picked)
                if c < PEERS - 1:
                    right = ref[i, :, (2 * c + 2) * LANES : (2 * c + 3) * LANES].astype(F32)
                    picked = jnp.where(lane < REACH, right, picked)
                edges = edges + pltpu.roll(picked, (2 * a + i) * 8 + REACH, 1)
        edges = pltpu.roll(edges, turn, 1)
        out_ref[c, EDGE_ROW:SEND_ROWS, :] = edges.astype(BF16)


def halo_kernel(where_ref, got_ref, near_ref, far_ref, wide, near, far):
    core = where_ref[1] % 2

    def take(index, source_row, target_row, height):
        low = wide[index, pl.ds(source_row + core * (ROWS - height), height), :]
        high = wide[index, pl.ds(source_row + (1 - core) * (ROWS - height), height), :]
        far[target_row : target_row + height, :] = low
        near[target_row : target_row + height, :] = high

    for k in range(PEERS):
        wide[k] = got_ref[k, :EDGE_ROW, :].astype(F32)
    for half in range(2):
        total = got_ref[4 * half, EDGE_ROW:SEND_ROWS, :].astype(F32)
        for k in range(4 * half + 1, 4 * half + 4):
            total = total + got_ref[k, EDGE_ROW:SEND_ROWS, :].astype(F32)
        wide[PEERS, half * ROWS : (half + 1) * ROWS, :] = total
    for j in range(EPOCHS):
        for a in range(2):
            for t in range(2):
                row = ((a * 2 + j % 2) * 2 + t) * ROWS
                take(j // 2, row, (a * 2 + t) * HALO_ROWS + HALO_AT[j], HALO[j])
    take(PEERS, 0, EDGE_LO_AT, EDGE_LO)
    take(PEERS, ROWS, EDGE_HI_AT, EDGE_HI)
    rest = EDGE_HI_AT + EDGE_HI
    near[rest:HALO_SEND, :] = jnp.zeros((HALO_SEND - rest, LANES), F32)
    far[rest:HALO_SEND, :] = jnp.zeros((HALO_SEND - rest, LANES), F32)
    near_ref[...] = near[...].astype(BF16)
    far_ref[...] = far[...].astype(BF16)


def split(values):
    high = values.astype(BF16)
    return high, (values - high.astype(F32)).astype(BF16)


def column_filter(image, variance, taps, count):
    high, low = split(image * variance)
    variance = variance.astype(BF16)

    def dot(left, right):
        return jnp.dot(left, right, preferred_element_type=F32)

    psi = dot(high, taps[0]) + (dot(low, taps[0]) + dot(high, taps[1]))
    phi = dot(variance, taps[2]) + dot(variance, taps[3])
    return psi, phi


def own_kernel(cols_ref, got_ref, out_ref, taps_ref, image, variance):
    shape = (COLS + LANES, COLS)
    place = lax.broadcasted_iota(jnp.int32, shape, 0)
    place = jnp.where(place < COLS + LANES // 2, place, place - (COLS + LANES))
    step = place - lax.broadcasted_iota(jnp.int32, shape, 1) + REACH
    psi_taps = jnp.zeros(shape, F32)
    phi_taps = jnp.zeros(shape, F32)
    for b in range(PSF):
        hit = step == b
        psi_taps = jnp.where(hit, cols_ref[b], psi_taps)
        phi_taps = jnp.where(hit, cols_ref[b] * cols_ref[b], phi_taps)
    taps_ref[0], taps_ref[1] = split(psi_taps)
    taps_ref[2], taps_ref[3] = split(phi_taps)
    edges = []
    for half in range(2):
        total = got_ref[4 * half, EDGE_ROW:SEND_ROWS, :].astype(F32)
        for k in range(4 * half + 1, 4 * half + 4):
            total = total + got_ref[k, EDGE_ROW:SEND_ROWS, :].astype(F32)
        edges.append(total)
    for j in range(EPOCHS):
        for a, ref in enumerate((image, variance)):
            for t in range(2):
                row = ((a * 2 + j % 2) * 2 + t) * ROWS
                ref[j * ROWS : (j + 1) * ROWS, t * LANES : (t + 1) * LANES] = got_ref[
                    j // 2, row : row + ROWS, :
                ].astype(F32)
            turn = (LANES - REACH - edge_lane(a, j)) % LANES
            ref[j * ROWS : (j + 1) * ROWS, COLS:] = pltpu.roll(edges[j // 8], turn, 1)
    psi, phi = column_filter(image[...], variance[...], taps_ref, EPOCHS)
    for j in range(EPOCHS):
        rows = slice(j * ROWS, (j + 1) * ROWS)
        for t in range(2):
            lanes = slice(t * LANES, (t + 1) * LANES)
            out_ref[j, t] = psi[rows, lanes]
            out_ref[j, 2 + t] = phi[rows, lanes]


def stack_kernel(
    where_ref,
    rows_ref,
    shift_ref,
    own_ref,
    taps_ref,
    near_ref,
    far_ref,
    out_ref,
    wide,
    image,
    variance,
    filtered,
    maps,
    first,
    second,
):
    sky = where_ref[1]
    core = sky % 2
    wide[core] = near_ref[...].astype(F32)
    wide[1 - core] = far_ref[...].astype(F32)
    for side in range(2):
        source = 1 - side
        for a, ref in enumerate((image, variance)):
            for t in range(2):
                start = (a * 2 + t) * HALO_ROWS
                ref[side * HALO_ROWS : (side + 1) * HALO_ROWS, t * LANES : (t + 1) * LANES] = wide[
                    source, start : start + HALO_ROWS, :
                ]
            for j in range(EPOCHS):
                start, height = (EDGE_LO_AT, EDGE_LO) if j < 8 else (EDGE_HI_AT, EDGE_HI)
                if side == 0:
                    start = start + height - HALO[j]
                turn = (LANES - REACH - edge_lane(a, j)) % LANES
                row = side * HALO_ROWS + HALO_AT[j]
                ref[row : row + HALO[j], COLS:] = pltpu.roll(wide[source, start : start + HALO[j], :], turn, 1)
    psi, phi = column_filter(image[...], variance[...], taps_ref, EPOCHS)
    for t in range(2):
        lanes = slice(t * LANES, (t + 1) * LANES)
        filtered[t] = psi[:, lanes]
        filtered[2 + t] = phi[:, lanes]
    for j in range(EPOCHS):
        for p in range(4):
            above = HALO_AT[j]
            below = HALO_ROWS + HALO_AT[j]
            maps[j, p, BASE - HALO[j] : BASE, :] = filtered[p, above : above + HALO[j], :]
            maps[j, p, BASE : BASE + ROWS, :] = own_ref[j, p]
            maps[j, p, BASE + ROWS : BASE + ROWS + HALO[j], :] = filtered[p, below : below + HALO[j], :]

    def chunks(reach):
        return range((BASE - reach) // 8 * 8, BASE + ROWS + reach, 8)

    row_taps = [[rows_ref[a] for a in range(PSF)], [rows_ref[a] * rows_ref[a] for a in range(PSF)]]

    for j in range(EPOCHS):
        for m in range(2):

            def filter_rows(t, carry, j=j, m=m):
                p = 2 * m + t
                for r in chunks(2 * j):
                    total = row_taps[m][0] * maps[j, p, r - REACH : r - REACH + 8, :]
                    for a in range(1, PSF):
                        total = total + row_taps[m][a] * maps[j, p, r - REACH + a : r - REACH + a + 8, :]
                    first[j, p, r : r + 8, :] = total
                return carry

            lax.fori_loop(0, 2, filter_rows, 0)

    def clear(ref):
        @pl.when(sky == 0)
        def _():
            ref[:, :, :BASE, :] = jnp.zeros((EPOCHS, 4, BASE, LANES), F32)

        @pl.when(sky == sky_last)
        def _():
            ref[:, :, BASE + ROWS :, :] = jnp.zeros((EPOCHS, 4, SPAN - BASE - ROWS, LANES), F32)

    sky_last = where_ref[2] - 1
    clear(first)

    def moves(level, j):
        number = shift_ref[level, j]
        whole = lax.shift_right_arithmetic(number, 2)
        part = number - whole * 4
        fraction = part.astype(F32) * 0.25
        behind = jnp.where(part > 0, whole + 1, whole)
        return whole, behind, 1.0 - fraction, fraction

    def shifted(ref, k, p, r, move):
        whole, behind, keep, fraction = move
        return keep * ref[k, p, pl.ds(r - whole, 8), :] + fraction * ref[k, p, pl.ds(r - behind, 8), :]

    source, target = first, second
    for level in range(LEVELS - 1):
        span = 1 << level
        for low in range(EPOCHS):
            if low & span:
                continue
            high = low + span
            reach = 2 * (low >> (level + 1) << (level + 1))
            to_low, to_high = moves(level, low), moves(level, high)

            def step(p, carry, low=low, high=high, reach=reach, to_low=to_low, to_high=to_high, source=source, target=target):
                for r in chunks(reach):
                    base = source[low, p, r : r + 8, :]
                    target[low, p, r : r + 8, :] = base + shifted(source, high, p, r, to_low)
                    target[high, p, r : r + 8, :] = base + shifted(source, high, p, r, to_high)
                return carry

            lax.fori_loop(0, 4, step, 0)
        clear(target)
        source, target = target, source

    level = LEVELS - 1
    span = 1 << level
    last_moves = [(moves(level, low), moves(level, low + span)) for low in range(span)]
    for t in range(2):
        for r in range(BASE, BASE + ROWS, 8):
            values = []
            for low in range(span):
                high = low + span
                for move in last_moves[low]:
                    psi = source[low, t, r : r + 8, :] + shifted(source, high, t, r, move)
                    phi = source[low, 2 + t, r : r + 8, :] + shifted(source, high, 2 + t, r, move)
                    values.append(psi * lax.rsqrt(phi))
            peak = values[0]
            for value in values[1:]:
                peak = jnp.maximum(peak, value)
            total = jnp.exp(values[0] - peak)
            for value in values[1:]:
                total = total + jnp.exp(value - peak)
            out_ref[r - BASE : r - BASE + 8, t * LANES : (t + 1) * LANES] = peak + jnp.log(total)


def smem():
    return pl.BlockSpec(memory_space=pltpu.SMEM)


def vmem():
    return pl.BlockSpec(memory_space=pltpu.VMEM)


def limits():
    return pltpu.CompilerParams(vmem_limit_bytes=48 * 1024 * 1024)


def on_device(image, inv_variance, psf_rows, psf_cols, shift_num):
    sky_count = lax.axis_size("sky")
    where = jnp.stack([lax.axis_index("epoch"), lax.axis_index("sky"), sky_count]).astype(jnp.int32)
    packed = pl.pallas_call(
        pack_kernel,
        out_shape=jax.ShapeDtypeStruct((PEERS, SEND_ROWS, LANES), BF16),
        in_specs=[smem(), vmem(), vmem()],
        out_specs=vmem(),
        compiler_params=limits(),
        name="pack",
    )(where, image, inv_variance)
    got = lax.all_to_all(packed, "epoch", 0, 0, tiled=True)
    halo_shape = jax.ShapeDtypeStruct((HALO_SEND, LANES), BF16)
    near, far = pl.pallas_call(
        halo_kernel,
        out_shape=(halo_shape, halo_shape),
        in_specs=[smem(), vmem()],
        out_specs=(vmem(), vmem()),
        scratch_shapes=[
            pltpu.VMEM((PEERS + 1, EDGE_ROW, LANES), F32),
            pltpu.VMEM((HALO_SEND, LANES), F32),
            pltpu.VMEM((HALO_SEND, LANES), F32),
        ],
        compiler_params=limits(),
        name="halo",
    )(where, got)
    far = lax.ppermute(far, "sky", [(i, i + 1) if i % 2 else (i, i - 1) for i in range(1, sky_count - 1)])
    near = lax.ppermute(near, "sky", [(i, i ^ 1) for i in range(sky_count)])
    own, taps = pl.pallas_call(
        own_kernel,
        out_shape=(
            jax.ShapeDtypeStruct((EPOCHS, 4, ROWS, LANES), F32),
            jax.ShapeDtypeStruct((4, COLS + LANES, COLS), BF16),
        ),
        in_specs=[smem(), vmem()],
        out_specs=(vmem(), vmem()),
        scratch_shapes=[pltpu.VMEM((EPOCHS * ROWS, COLS + LANES), F32)] * 2,
        compiler_params=limits(),
        cost_estimate=pl.CostEstimate(flops=1_000_000_000, bytes_accessed=8_000_000, transcendentals=0),
        name="own",
    )(psf_cols, got)
    return pl.pallas_call(
        stack_kernel,
        out_shape=jax.ShapeDtypeStruct((ROWS, COLS), F32),
        in_specs=[smem(), smem(), smem(), vmem(), vmem(), vmem(), vmem()],
        out_specs=vmem(),
        scratch_shapes=[
            pltpu.VMEM((2, HALO_SEND, LANES), F32),
            pltpu.VMEM((2 * HALO_ROWS, COLS + LANES), F32),
            pltpu.VMEM((2 * HALO_ROWS, COLS + LANES), F32),
            pltpu.VMEM((4, 2 * HALO_ROWS, LANES), F32),
            pltpu.VMEM((EPOCHS, 4, SPAN, LANES), F32),
            pltpu.VMEM((EPOCHS, 4, SPAN, LANES), F32),
            pltpu.VMEM((EPOCHS, 4, SPAN, LANES), F32),
        ],
        compiler_params=limits(),
        cost_estimate=pl.CostEstimate(flops=1_000_000_000, bytes_accessed=8_000_000, transcendentals=400_000),
        name="stack",
    )(where, psf_rows, shift_num, own, taps, near, far)


def solution(mesh):
    return jax.shard_map(
        on_device,
        mesh=mesh,
        in_specs=(P("epoch", "sky", None), P("epoch", "sky", None), P(), P(), P()),
        out_specs=P("sky", "epoch"),
        check_vma=False,
    )
```

time: 447 us -> 46.1 us (0.10)
  waiting for transfers between devices: 279 us -> 7 us
  other arithmetic: 52.5 us -> 0.08 us
  between operations: 42.2 us -> 0.06 us
  starting transfers between devices: 40 us -> 6.8 us
  local copies, waits for them, and re-layouts: 28.8 us -> 2.01 us
  blocking collectives: 0 us -> 17.4 us
  Pallas kernels: 0 us -> 12.5 us
    all_gather x2 -> x0, waiting for transfers between devices: 147 us -> none  [combined_all(): everything = jax.tree.map(lambda part: lax.all_gather(part, axis), x)]
    ppermute x13 -> x2, waiting for transfers between devices: 131 us -> 7 us  [the longest x1 7 us: on_device(): lax.ppermute(far, 'sky', [(i, i + 1) if i % 2 else (i, i - 1) for i in ra...]
    ppermute x13 -> x2, starting transfers between devices: 40 us -> 6.8 us  [the longest x1 4.45 us: on_device(): lax.ppermute(far, 'sky', [(i, i + 1) if i % 2 else (i, i - 1) for i in ra...]
    add x14 -> x0, other arithmetic: 27.7 us -> none  [the longest x7 10.2 us: combine_pairs(): first[1] * jnp.exp(first[0] - top_value)]
    all_to_all x0 -> x1, blocking collectives: none -> 17.4 us  [on_device(): got = lax.all_to_all(packed, 'epoch', 0, 0, tiled=True)]
    pallas_call x0 -> x4, Pallas kernels: none -> 12.5 us  [the longest x1 8.74 us: on_device(): pl.pallas_call(stack_kernel, out_shape=jax.ShapeDtypeStruct((ROWS, COLS),...]
    gather x3 -> x0, local copies, waits for them, and re-layouts: 11.7 us -> none  [take_rows(): return lax.dynamic_slice_in_dim(one_block, start, row_count + 1, axis=1)]
    another operation x2 -> x1, other arithmetic: 9.08 us -> 0.08 us  [on_device(): jnp.stack([lax.axis_index('epoch'), lax.axis_index('sky'), sky_count])]
  transfers between devices with their start and end apart: 15 -> 2, of which waited for: 11 -> 1; matrix products, arithmetic and copies ran while one was open for 1% -> 0% of each run, Pallas kernels for 0% -> 4%
where the time goes in v1:
time: 46.1 us; the launch traced here: 45.9 us
  blocking collectives  17.4 us (38%)
  Pallas kernels  12.5 us (27%)
  waiting for transfers between devices  7 us (15%)
  starting transfers between devices  6.8 us (15%)
  local copies, waits for them, and re-layouts  2.01 us (4%)
    all_to_all x1, blocking collectives, on_device(): got = lax.all_to_all(packed, 'epoch', 0, 0, tiled=True)  17.4 us
    pallas_call x1, Pallas kernels, on_device(): pl.pallas_call(stack_kernel, out_shape=jax.ShapeDtypeStruct((ROWS, COLS),...  8.74 us
    ppermute x1, waiting for transfers between devices, on_device(): lax.ppermute(far, 'sky', [(i, i + 1) if i % 2 else (i, i - 1) for i in ra...  7 us
    ppermute x1, starting transfers between devices, on_device(): lax.ppermute(far, 'sky', [(i, i + 1) if i % 2 else (i, i - 1) for i in ra...  4.45 us
    ppermute x1, starting transfers between devices, on_device(): near = lax.ppermute(near, 'sky', [(i, i ^ 1) for i in range(sky_count)])  2.35 us
    pallas_call x1, Pallas kernels, on_device(): pl.pallas_call(own_kernel, out_shape=(jax.ShapeDtypeStruct((EPOCHS, 4, RO...  2.04 us
    unnamed x10, local copies, waits for them, and re-layouts  2.01 us
  transfers between devices with their start and end apart: 2, of which 1 were waited for; matrix products, arithmetic and copies ran while one was open for 0% of the time, Pallas kernels for 4%

profile of v1, /device:TPU:129, one launch (start us, length us, event | category | flops | bytes accessed | tf_op | source)
XLA Modules:
  0.0 45.9 jit_solution(8902637111662573578)
XLA Ops:
  0.0 0.1 pad_add_fusion.where_ref
  0.1 0.0 copy-start
  0.1 1.0 %copy-done = bf16[2,48,2048]{2,1,0:T(8,128)(2,1)S(1)} copy-done((bf16[2,48,2048]{2,1,0:T(8,128)(2,1)S(1)}, bf16[2,48,2048]{2,1,0:T(8,128)(2,1)}, u32[]{:S(2)}) %copy-start) | copy-done | bytes 393240
  1.1 0.0 copy-start.1
  1.1 1.0 %copy-done.1 = bf16[2,48,2048]{2,1,0:T(8,128)(2,1)S(1)} copy-done((bf16[2,48,2048]{2,1,0:T(8,128)(2,1)S(1)}, bf16[2,48,2048]{2,1,0:T(8,128)(2,1)}, u32[]{:S(2)}) %copy-start.1) | copy-done | bytes 393240
  2.1 0.9 %pack.1 = bf16[8,432,128]{2,1,0:T(8,128)(2,1)S(1)} custom-call(s32[3]{0:T(128)S(1)} %pad_add_fusion.where_ref, bf16[2,48,2048]{2,1,0:T(8,128)(2,1)S(1)} %copy-done, bf16[2,48,2048]{2,1,0:T(8,128)(2,1)S(1)} %copy-done.1), custom_call_target="tpu_custom_call" | custom-call | tf_op jit(solution)/shard_map/pack/pallas_call | solution.py:291
  3.0 0.0 copy-start.3
  3.0 17.4 %all_to_all.5.got_ref = bf16[8,432,128]{2,1,0:T(8,128)(2,1)S(1)} all-to-all(bf16[8,432,128]{2,1,0:T(8,128)(2,1)S(1)} %pack.1), channel_id=1, replica_groups=mesh['epoch'=8,'sky'=32] {'epoch'}, dimensions={0} | all-to-all | bytes 1769472 | tf_op jit(solution)/shard_map/all_to_all | solution.py:299
  20.4 0.8 %halo.1 = (bf16[1280,128]{1,0:T(8,128)(2,1)S(1)}, bf16[1280,128]{1,0:T(8,128)(2,1)S(1)}) custom-call(s32[3]{0:T(128)S(1)} %pad_add_fusion.where_ref, bf16[8,432,128]{2,1,0:T(8,128)(2,1)S(1)} %all_to_all.5.got_ref), custom_call_target="tpu_custom_call" | custom-call | tf_op jit(solution)/shard_map/halo/pallas_call | solution.py:301
  21.2 2.4 %collective-permute-start = (bf16[1280,128]{1,0:T(8,128)(2,1)S(1)}, bf16[1280,128]{1,0:T(8,128)(2,1)S(1)}, u32[]{:S(2)}, u32[]{:S(2)}) collective-permute-start(bf16[1280,128]{1,0:T(8,128)(2,1)S(1)} %get-tuple-element.11), channel_id=1, source_target_pairs={{0,1},{1,0},{2,3},{3,2},{4,5},{5,4},{6,7},{7,6},{8,9},{9,8},{10,11... | collective-permute-start | bytes 983048 | tf_op jit(solution)/shard_map/ppermute | solution.py:315
  23.6 0.0 copy-start.2
  23.6 0.0 copy-start.4
  23.6 4.4 %collective-permute-start.1 = (bf16[1280,128]{1,0:T(8,128)(2,1)S(1)}, bf16[1280,128]{1,0:T(8,128)(2,1)S(1)}, u32[]{:S(2)}, u32[]{:S(2)}) collective-permute-start(bf16[1280,128]{1,0:T(8,128)(2,1)S(1)} %get-tuple-element.12), channel_id=1, source_target_pairs={{1,2},{2,1},{3,4},{4,3},{5,6},{6,5},{7,8},{8,7},{9,10},{10,9},{11,... | collective-permute-start | bytes 983048 | tf_op jit(solution)/shard_map/ppermute | solution.py:314
  28.1 0.0 copy-done.3
  28.1 2.0 %own.1 = (f32[16,4,48,128]{3,2,1,0:T(8,128)S(1)}, bf16[4,384,256]{2,1,0:T(8,128)(2,1)S(1)}) custom-call(f32[9]{0:T(128)S(1)} %copy-done.3, bf16[8,432,128]{2,1,0:T(8,128)(2,1)S(1)} %all_to_all.5.got_ref), custom_call_target="tpu_custom_call" | custom-call | flops 1000000000 | bytes 8000000 | tf_op jit(solution)/shard_map/own/pallas_call | solution.py:316
  30.1 0.0 collective-permute-done.near_ref
  30.1 7.0 %collective-permute-done.1.far_ref = bf16[1280,128]{1,0:T(8,128)(2,1)S(1)} collective-permute-done((bf16[1280,128]{1,0:T(8,128)(2,1)S(1)}, bf16[1280,128]{1,0:T(8,128)(2,1)S(1)}, u32[]{:S(2)}, u32[]{:S(2)}) %collective-permute-start.1) | collective-permute-done | bytes 327712 | tf_op jit(solution)/shard_map/ppermute | solution.py:314
  37.1 0.0 copy-done.2
  37.1 0.0 copy-done.4
  37.1 8.7 %stack.13 = f32[48,256]{1,0:T(8,128)} custom-call(s32[3]{0:T(128)S(1)} %pad_add_fusion.where_ref, f32[9]{0:T(128)S(1)} %copy-done.4, s32[4,16]{1,0:T(4,128)S(1)} %copy-done.2, f32[16,4,48,128]{3,2,1,0:T(8,128)S(1)} %get-tuple-element.9.own_ref, bf16[4,384,256]{2,1,0:T(8,128)(2,1)S(1)} %get-tuple-element.10.taps_ref, ...), custom_call_target="tpu_custom_call" | custom-call | flops 1000000000 | bytes 8000000 | tf_op jit(solution)/shard_map/stack/pallas_call | solution.py:329
Async XLA Ops:
  0.1 1.0 %copy-start = (bf16[2,48,2048]{2,1,0:T(8,128)(2,1)S(1)}, bf16[2,48,2048]{2,1,0:T(8,128)(2,1)}, u32[]{:S(2)}) copy-start(bf16[2,48,2048]{2,1,0:T(8,128)(2,1)} %image_ref.1) | copy-start | bytes 1179652
  1.1 1.0 %copy-start.1 = (bf16[2,48,2048]{2,1,0:T(8,128)(2,1)S(1)}, bf16[2,48,2048]{2,1,0:T(8,128)(2,1)}, u32[]{:S(2)}) copy-start(bf16[2,48,2048]{2,1,0:T(8,128)(2,1)} %variance_ref.1) | copy-start | bytes 1179652
  3.0 25.1 %copy-start.3 = (f32[9]{0:T(128)S(1)}, f32[9]{0:T(128)}, u32[]{:S(2)}) copy-start(f32[9]{0:T(128)} %cols_ref.1) | copy-start | bytes 112
  21.2 8.9 %collective-permute-start = (bf16[1280,128]{1,0:T(8,128)(2,1)S(1)}, bf16[1280,128]{1,0:T(8,128)(2,1)S(1)}, u32[]{:S(2)}, u32[]{:S(2)}) collective-permute-start(bf16[1280,128]{1,0:T(8,128)(2,1)S(1)} %get-tuple-element.11), channel_id=1, source_target_pairs={{0,1},{1,0},{2,3},{3,2},{4,5},{5,4},{6,7},{7,6},{8,9},{9,8},{10,11... | collective-permute-start | bytes 983048 | tf_op jit(solution)/shard_map/ppermute | solution.py:315
  23.6 13.5 %copy-start.2 = (s32[4,16]{1,0:T(4,128)S(1)}, s32[4,16]{1,0:T(4,128)}, u32[]{:S(2)}) copy-start(s32[4,16]{1,0:T(4,128)} %shift_ref.1) | copy-start | bytes 772
  23.6 13.5 %copy-start.4 = (f32[9]{0:T(128)S(1)}, f32[9]{0:T(128)}, u32[]{:S(2)}) copy-start(f32[9]{0:T(128)} %rows_ref.1) | copy-start | bytes 112
  23.6 13.5 %collective-permute-start.1 = (bf16[1280,128]{1,0:T(8,128)(2,1)S(1)}, bf16[1280,128]{1,0:T(8,128)(2,1)S(1)}, u32[]{:S(2)}, u32[]{:S(2)}) collective-permute-start(bf16[1280,128]{1,0:T(8,128)(2,1)S(1)} %get-tuple-element.12), channel_id=1, source_target_pairs={{1,2},{2,1},{3,4},{4,3},{5,6},{6,5},{7,8},{8,7},{9,10},{10,9},{11,... | collective-permute-start | bytes 983048 | tf_op jit(solution)/shard_map/ppermute | solution.py:314

commit v2 on v1

v2 whole, which is shorter than its diff:
```python
import functools

import jax
import jax.numpy as jnp
from jax import lax
from jax.experimental import pallas as pl
from jax.experimental.pallas import tpu as pltpu
from jax.sharding import PartitionSpec as P

EPOCHS = 16
LEVELS = 4
PSF = 9
REACH = 4
PEERS = 8
ROWS = 48
LANES = 128
COLS = 256
EDGE_ROW = 8 * ROWS
SEND_ROWS = 9 * ROWS
HALO = [2 * j + REACH for j in range(EPOCHS)]
HALO_AT = [sum(HALO[:j]) for j in range(EPOCHS)]
HALO_ROWS = sum(HALO)
EDGE_LO = HALO[7]
EDGE_HI = HALO[15]
EDGE_LO_AT = 4 * HALO_ROWS
EDGE_HI_AT = EDGE_LO_AT + EDGE_LO
HALO_SEND = 1280
BASE = 40
SPAN = 128
F32 = jnp.float32
BF16 = jnp.bfloat16


def edge_lane(array, j):
    return 32 * ((j // 2) % 4) + (2 * array + j % 2) * 8


def pack_kernel(image_hbm, variance_hbm, out_hbm, held, blocks, sums, edges, arrived, sent):
    turn = 32 * (lax.axis_index("epoch") % 4)
    lane = lax.broadcasted_iota(jnp.int32, (ROWS, LANES), 1)
    copies = []
    for a, ref in enumerate((image_hbm, variance_hbm)):
        for i in range(2):
            copies.append(pltpu.make_async_copy(ref.at[i], held.at[2 * a + i], arrived.at[2 * a + i]))
            copies[-1].start()

    def edge(b, c):
        picked = jnp.zeros((ROWS, LANES), F32)
        if c > 0:
            left = held[b, :, (2 * c - 1) * LANES : 2 * c * LANES].astype(F32)
            picked = jnp.where(lane >= LANES - REACH, left, picked)
        if c < PEERS - 1:
            right = held[b, :, (2 * c + 2) * LANES : (2 * c + 3) * LANES].astype(F32)
            picked = jnp.where(lane < REACH, right, picked)
        return pltpu.roll(picked, b * 8 + REACH, 1)

    out = []

    def send(source, n, row, height):
        out.append(pltpu.make_async_copy(source, out_hbm.at[:, pl.ds(row, height), :], sent.at[n]))
        out[-1].start()

    for b in range(4):
        copies[b].wait()
        for c in range(PEERS):
            for t in range(2):
                lanes = slice((2 * c + t) * LANES, (2 * c + t + 1) * LANES)
                blocks[b, c, t * ROWS : (t + 1) * ROWS, :] = held[b, :, lanes]
        send(blocks.at[b], b, 2 * b * ROWS, 2 * ROWS)
        for c in range(PEERS):
            total = edge(b, c)
            if b > 0:
                total = total + sums[c]
            if b < 3:
                sums[c] = total
            else:
                edges[c] = pltpu.roll(total, turn, 1).astype(BF16)
    send(edges, 4, EDGE_ROW, ROWS)
    for copy in out:
        copy.wait()


def build_halo(to_far, got_ref, out_ref, wide, out):
    core = lax.axis_index("sky") % 2
    last = core if to_far else 1 - core

    def take(index, source_row, target_row, height):
        start = source_row + last * (ROWS - height)
        out[target_row : target_row + height, :] = wide[index, pl.ds(start, height), :]

    for k in range(PEERS):
        wide[k] = got_ref[k, :EDGE_ROW, :].astype(F32)
    for half in range(2):
        total = got_ref[4 * half, EDGE_ROW:SEND_ROWS, :].astype(F32)
        for k in range(4 * half + 1, 4 * half + 4):
            total = total + got_ref[k, EDGE_ROW:SEND_ROWS, :].astype(F32)
        wide[PEERS, half * ROWS : (half + 1) * ROWS, :] = total
    for j in range(EPOCHS):
        for a in range(2):
            for t in range(2):
                row = ((a * 2 + j % 2) * 2 + t) * ROWS
                take(j // 2, row, (a * 2 + t) * HALO_ROWS + HALO_AT[j], HALO[j])
    take(PEERS, 0, EDGE_LO_AT, EDGE_LO)
    take(PEERS, ROWS, EDGE_HI_AT, EDGE_HI)
    rest = EDGE_HI_AT + EDGE_HI
    out[rest:HALO_SEND, :] = jnp.zeros((HALO_SEND - rest, LANES), F32)
    out_ref[...] = out[...].astype(BF16)


def split(values):
    high = values.astype(BF16)
    return high, (values - high.astype(F32)).astype(BF16)


def column_filter(image, variance, taps):
    high, low = split(image * variance)
    variance = variance.astype(BF16)

    def dot(left, right):
        return jnp.dot(left, right, preferred_element_type=F32)

    psi = dot(high, taps[0]) + (dot(low, taps[0]) + dot(high, taps[1]))
    phi = dot(variance, taps[2]) + dot(variance, taps[3])
    return psi, phi


def own_kernel(cols_ref, got_ref, out_ref, taps_ref, image, variance):
    shape = (COLS + LANES, COLS)
    place = lax.broadcasted_iota(jnp.int32, shape, 0)
    place = jnp.where(place < COLS + LANES // 2, place, place - (COLS + LANES))
    step = place - lax.broadcasted_iota(jnp.int32, shape, 1) + REACH
    psi_taps = jnp.zeros(shape, F32)
    phi_taps = jnp.zeros(shape, F32)
    for b in range(PSF):
        hit = step == b
        psi_taps = jnp.where(hit, cols_ref[b], psi_taps)
        phi_taps = jnp.where(hit, cols_ref[b] * cols_ref[b], phi_taps)
    taps_ref[0], taps_ref[1] = split(psi_taps)
    taps_ref[2], taps_ref[3] = split(phi_taps)
    edges = []
    for half in range(2):
        total = got_ref[4 * half, EDGE_ROW:SEND_ROWS, :].astype(F32)
        for k in range(4 * half + 1, 4 * half + 4):
            total = total + got_ref[k, EDGE_ROW:SEND_ROWS, :].astype(F32)
        edges.append(total)
    for j in range(EPOCHS):
        for a, ref in enumerate((image, variance)):
            for t in range(2):
                row = ((a * 2 + j % 2) * 2 + t) * ROWS
                ref[j * ROWS : (j + 1) * ROWS, t * LANES : (t + 1) * LANES] = got_ref[
                    j // 2, row : row + ROWS, :
                ].astype(F32)
            turn = (LANES - REACH - edge_lane(a, j)) % LANES
            ref[j * ROWS : (j + 1) * ROWS, COLS:] = pltpu.roll(edges[j // 8], turn, 1)
    psi, phi = column_filter(image[...], variance[...], taps_ref)
    for j in range(EPOCHS):
        rows = slice(j * ROWS, (j + 1) * ROWS)
        for t in range(2):
            lanes = slice(t * LANES, (t + 1) * LANES)
            out_ref[j, t] = psi[rows, lanes]
            out_ref[j, 2 + t] = phi[rows, lanes]


def put_halo(above, wide, taps_ref, image, variance, filtered, maps):
    for a, ref in enumerate((image, variance)):
        for t in range(2):
            start = (a * 2 + t) * HALO_ROWS
            ref[:, t * LANES : (t + 1) * LANES] = wide[start : start + HALO_ROWS, :]
        for j in range(EPOCHS):
            start, height = (EDGE_LO_AT, EDGE_LO) if j < 8 else (EDGE_HI_AT, EDGE_HI)
            start = start + above * (height - HALO[j])
            turn = (LANES - REACH - edge_lane(a, j)) % LANES
            ref[HALO_AT[j] : HALO_AT[j] + HALO[j], COLS:] = pltpu.roll(wide[pl.ds(start, HALO[j]), :], turn, 1)
    psi, phi = column_filter(image[...], variance[...], taps_ref)
    for t in range(2):
        lanes = slice(t * LANES, (t + 1) * LANES)
        filtered[t] = psi[:, lanes]
        filtered[2 + t] = phi[:, lanes]
    for j in range(EPOCHS):
        start = jnp.where(above == 1, BASE - HALO[j], BASE + ROWS)
        for p in range(4):
            maps[j, p, pl.ds(start, HALO[j]), :] = filtered[p, HALO_AT[j] : HALO_AT[j] + HALO[j], :]


def slot(level, j):
    done = j & ((1 << level) - 1)
    if not done:
        return j
    b = done.bit_length() - 1
    return EPOCHS + 8 * b + ((j >> (b + 1)) << b | (j & ((1 << b) - 1)))


def moves(shift_ref, level, j):
    number = shift_ref[level, j]
    whole = lax.shift_right_arithmetic(number, 2)
    part = number - whole * 4
    fraction = part.astype(F32) * 0.25
    behind = jnp.where(part > 0, whole + 1, whole)
    return whole, behind, 1.0 - fraction, fraction


def shifted(ref, place, p, r, height, move):
    whole, behind, keep, fraction = move
    return keep * ref[place, p, pl.ds(r - whole, height), :] + fraction * ref[place, p, pl.ds(r - behind, height), :]


EDGE = [REACH, REACH + 2, REACH + 6, REACH + 14]


def span_of(core, level, reach, far):
    height = EDGE[level] + reach if far else ROWS - EDGE[level] + reach
    count = -(-height // 8)
    top, bottom = BASE + EDGE[level], BASE + ROWS - EDGE[level]
    if far:
        return jnp.where(core == 0, top - 8 * count, bottom), count
    return jnp.where(core == 0, top, bottom - 8 * count), count


def filter_rows(core, far, rows_ref, maps, stacks):
    taps = [[rows_ref[a] for a in range(PSF)], [rows_ref[a] * rows_ref[a] for a in range(PSF)]]
    for j in range(EPOCHS):
        start, count = span_of(core, 0, 2 * j, far)
        for m in range(2):

            def one(t, carry, j=j, m=m, start=start, count=count):
                p = 2 * m + t
                total = taps[m][0] * maps[j, p, pl.ds(start - REACH, 8 * count), :]
                for a in range(1, PSF):
                    total = total + taps[m][a] * maps[j, p, pl.ds(start - REACH + a, 8 * count), :]
                stacks[j, p, pl.ds(start, 8 * count), :] = total
                return carry

            lax.fori_loop(0, 2, one, 0)


BATCH = 12


def run_level(core, far, level, shift_ref, stacks):
    held, size = [], 0

    def store():
        for place, p, rows, value in held:
            stacks[place, p, rows, :] = value
        held.clear()

    for low in range(EPOCHS):
        if low >> level & 1:
            continue
        high = low + (1 << level)
        reach = 2 * (low >> (level + 1) << (level + 1))
        start, count = span_of(core, level + 1, reach, far)
        rows = pl.ds(start, 8 * count)
        to_low, to_high = moves(shift_ref, level, low), moves(shift_ref, level, high)
        from_at = slot(level, high)
        for p in range(4):
            if size + count > BATCH:
                store()
                size = 0
            base = stacks[slot(level, low), p, rows, :]
            for place, move in ((slot(level + 1, low), to_low), (slot(level + 1, high), to_high)):
                held.append((place, p, rows, base + shifted(stacks, from_at, p, start, 8 * count, move)))
            size += count
    store()


def inner_kernel(
    rows_ref, shift_ref, own_ref, taps_ref, near_ref, stacks, wide, image, variance, filtered, maps
):
    core = lax.axis_index("sky") % 2
    wide[...] = near_ref[...].astype(F32)
    put_halo(core, wide, taps_ref, image, variance, filtered, maps)
    for j in range(EPOCHS):
        for p in range(4):
            maps[j, p, BASE : BASE + ROWS, :] = own_ref[j, p]
    filter_rows(core, False, rows_ref, maps, stacks)
    for level in range(LEVELS - 1):
        run_level(core, False, level, shift_ref, stacks)


def outer_kernel(
    rows_ref,
    shift_ref,
    own_ref,
    taps_ref,
    far_ref,
    stacks_in,
    out_ref,
    stacks,
    wide,
    image,
    variance,
    filtered,
    maps,
    values,
):
    sky = lax.axis_index("sky")
    sky_last = lax.axis_size("sky") - 1
    core = sky % 2

    def clear(level):
        @pl.when(sky == 0)
        def _():
            for j in range(EPOCHS):
                stacks[slot(level, j), :, :BASE, :] = jnp.zeros((4, BASE, LANES), F32)

        @pl.when(sky == sky_last)
        def _():
            for j in range(EPOCHS):
                stacks[slot(level, j), :, BASE + ROWS :, :] = jnp.zeros((4, SPAN - BASE - ROWS, LANES), F32)

    wide[...] = far_ref[...].astype(F32)
    put_halo(1 - core, wide, taps_ref, image, variance, filtered, maps)
    own_rows = core * (ROWS - 8)
    for j in range(EPOCHS):
        for p in range(4):
            maps[j, p, pl.ds(BASE + own_rows, 8), :] = own_ref[j, p, pl.ds(own_rows, 8), :]
    filter_rows(core, True, rows_ref, maps, stacks)
    clear(0)
    for level in range(LEVELS - 1):
        run_level(core, True, level, shift_ref, stacks)
        clear(level + 1)
    level = LEVELS - 1
    half = 1 << level
    last_moves = [(moves(shift_ref, level, low), moves(shift_ref, level, low + half)) for low in range(half)]
    for t in range(2):
        peak = None
        for low in range(half):
            base_at, from_at = slot(level, low), slot(level, low + half)
            psi_base = stacks[base_at, t, BASE : BASE + ROWS, :]
            phi_base = stacks[base_at, 2 + t, BASE : BASE + ROWS, :]
            for side, move in enumerate(last_moves[low]):
                psi = psi_base + shifted(stacks, from_at, t, BASE, ROWS, move)
                phi = phi_base + shifted(stacks, from_at, 2 + t, BASE, ROWS, move)
                value = psi * lax.rsqrt(phi)
                values[low + side * half] = value
                peak = value if peak is None else jnp.maximum(peak, value)
        total = jnp.exp(values[0] - peak)
        for v in range(1, EPOCHS):
            total = total + jnp.exp(values[v] - peak)
        out_ref[:, t * LANES : (t + 1) * LANES] = peak + jnp.log(total)


SLOTS = EPOCHS + 8 * (LEVELS - 1)


def smem():
    return pl.BlockSpec(memory_space=pltpu.SMEM)


def vmem():
    return pl.BlockSpec(memory_space=pltpu.VMEM)


def limits(mebibytes=32):
    return pltpu.CompilerParams(vmem_limit_bytes=mebibytes * 1024 * 1024)


def cost(microseconds):
    return pl.CostEstimate(flops=microseconds * 1_000_000_000, bytes_accessed=microseconds * 3_000_000, transcendentals=0)


def send_halo(to_far, got, name):
    return pl.pallas_call(
        functools.partial(build_halo, to_far),
        out_shape=jax.ShapeDtypeStruct((HALO_SEND, LANES), BF16),
        in_specs=[vmem()],
        out_specs=vmem(),
        scratch_shapes=[pltpu.VMEM((PEERS + 1, EDGE_ROW, LANES), F32), pltpu.VMEM((HALO_SEND, LANES), F32)],
        compiler_params=limits(),
        cost_estimate=cost(1),
        name=name,
    )(got)


def on_device(image, inv_variance, psf_rows, psf_cols, shift_num):
    sky_count = lax.axis_size("sky")
    cols = image.shape[2]
    packed = pl.pallas_call(
        pack_kernel,
        out_shape=jax.ShapeDtypeStruct((PEERS, SEND_ROWS, LANES), BF16),
        in_specs=[pl.BlockSpec(memory_space=pltpu.HBM), pl.BlockSpec(memory_space=pltpu.HBM)],
        out_specs=pl.BlockSpec(memory_space=pltpu.HBM),
        scratch_shapes=[
            pltpu.VMEM((4, ROWS, cols), BF16),
            pltpu.VMEM((4, PEERS, 2 * ROWS, LANES), BF16),
            pltpu.VMEM((PEERS, ROWS, LANES), F32),
            pltpu.VMEM((PEERS, ROWS, LANES), BF16),
            pltpu.SemaphoreType.DMA((4,)),
            pltpu.SemaphoreType.DMA((5,)),
        ],
        compiler_params=limits(60),
        cost_estimate=cost(2),
        name="pack",
    )(image, inv_variance)
    got = lax.all_to_all(packed, "epoch", 0, 0, tiled=True)
    near = send_halo(False, got, "near")
    near = lax.ppermute(near, "sky", [(i, i ^ 1) for i in range(sky_count)])
    far = send_halo(True, got, "far")
    far = lax.ppermute(far, "sky", [(i, i + 1) if i % 2 else (i, i - 1) for i in range(1, sky_count - 1)])
    own, taps = pl.pallas_call(
        own_kernel,
        out_shape=(
            jax.ShapeDtypeStruct((EPOCHS, 4, ROWS, LANES), F32),
            jax.ShapeDtypeStruct((4, COLS + LANES, COLS), BF16),
        ),
        in_specs=[smem(), vmem()],
        out_specs=(vmem(), vmem()),
        scratch_shapes=[pltpu.VMEM((EPOCHS * ROWS, COLS + LANES), F32)] * 2,
        compiler_params=limits(),
        cost_estimate=cost(5),
        name="own",
    )(psf_cols, got)
    stacks_shape = jax.ShapeDtypeStruct((SLOTS, 4, SPAN, LANES), F32)
    work = [
        pltpu.VMEM((HALO_SEND, LANES), F32),
        pltpu.VMEM((HALO_ROWS, COLS + LANES), F32),
        pltpu.VMEM((HALO_ROWS, COLS + LANES), F32),
        pltpu.VMEM((4, HALO_ROWS, LANES), F32),
        pltpu.VMEM((EPOCHS, 4, SPAN, LANES), F32),
    ]
    stacks = pl.pallas_call(
        inner_kernel,
        out_shape=stacks_shape,
        in_specs=[smem(), smem(), vmem(), vmem(), vmem()],
        out_specs=vmem(),
        scratch_shapes=work,
        compiler_params=limits(),
        cost_estimate=cost(5),
        name="inner",
    )(psf_rows, shift_num, own, taps, near)
    out, _ = pl.pallas_call(
        outer_kernel,
        out_shape=(jax.ShapeDtypeStruct((ROWS, COLS), F32), stacks_shape),
        in_specs=[smem(), smem(), vmem(), vmem(), vmem(), vmem()],
        out_specs=(vmem(), vmem()),
        scratch_shapes=[*work, pltpu.VMEM((EPOCHS, ROWS, LANES), F32)],
        input_output_aliases={5: 1},
        compiler_params=limits(),
        cost_estimate=cost(5),
        name="outer",
    )(psf_rows, shift_num, own, taps, far, stacks)
    return out


def solution(mesh):
    return jax.shard_map(
        on_device,
        mesh=mesh,
        in_specs=(P("epoch", "sky", None), P("epoch", "sky", None), P(), P(), P()),
        out_specs=P("sky", "epoch"),
        check_vma=False,
    )
```

time: 46.1 us -> 39.2 us (0.85)
  waiting for transfers between devices: 7 us -> 1.83 us
  local copies, waits for them, and re-layouts: 2.01 us -> 0.02 us
    ppermute x1, waiting for transfers between devices: 7 us -> 1.83 us  [on_device(): lax.ppermute(far, 'sky', [(i, i + 1) if i % 2 else (i, i - 1) for i in ra...]
    ppermute x1, starting transfers between devices: 2.35 us -> 0.09 us  [on_device(): near = lax.ppermute(near, 'sky', [(i, i ^ 1) for i in range(sky_count)])]
    ppermute x1, starting transfers between devices: 4.45 us -> 6.67 us  [on_device(): lax.ppermute(far, 'sky', [(i, i + 1) if i % 2 else (i, i - 1) for i in ra...]
    unnamed x10 -> x6, local copies, waits for them, and re-layouts: 2.01 us -> 0.02 us
    pallas_call x1, Pallas kernels: 0.9 us -> 2.2 us  [on_device(): pl.pallas_call(pack_kernel, out_shape=jax.ShapeDtypeStruct((PEERS, SEND_R...]
    pallas_call x2 -> x4, Pallas kernels: 9.57 us -> 8.48 us  [the longest x1 4.05 us: on_device(): pl.pallas_call(outer_kernel, out_shape=(jax.ShapeDtypeStruct((ROWS, COLS)...]
  transfers between devices with their start and end apart: 2 -> 2, of which waited for: 1 -> 1; matrix products, arithmetic and copies ran while one was open for 0% -> 0% of each run, Pallas kernels for 4% -> 16%
where the time goes in v2:
time: 39.2 us; the launch traced here: 39.1 us
  blocking collectives  17.6 us (45%)
  Pallas kernels  12.7 us (32%)
  starting transfers between devices  6.77 us (17%)
  waiting for transfers between devices  1.83 us (5%)
    all_to_all x1, blocking collectives, on_device(): got = lax.all_to_all(packed, 'epoch', 0, 0, tiled=True)  17.6 us
    ppermute x1, starting transfers between devices, on_device(): lax.ppermute(far, 'sky', [(i, i + 1) if i % 2 else (i, i - 1) for i in ra...  6.67 us
    pallas_call x1, Pallas kernels, on_device(): pl.pallas_call(outer_kernel, out_shape=(jax.ShapeDtypeStruct((ROWS, COLS)...  4.05 us
    pallas_call x1, Pallas kernels, on_device(): pl.pallas_call(inner_kernel, out_shape=stacks_shape, in_specs=[smem(), sm...  4.01 us
    pallas_call x1, Pallas kernels, on_device(): pl.pallas_call(pack_kernel, out_shape=jax.ShapeDtypeStruct((PEERS, SEND_R...  2.2 us
    pallas_call x1, Pallas kernels, on_device(): pl.pallas_call(own_kernel, out_shape=(jax.ShapeDtypeStruct((EPOCHS, 4, RO...  2.04 us
    ppermute x1, waiting for transfers between devices, on_device(): lax.ppermute(far, 'sky', [(i, i + 1) if i % 2 else (i, i - 1) for i in ra...  1.83 us
  transfers between devices with their start and end apart: 2, of which 1 were waited for; matrix products, arithmetic and copies ran while one was open for 0% of the time, Pallas kernels for 16%

profile of v2, /device:TPU:129, one launch (start us, length us, event | category | flops | bytes accessed | tf_op | source)
XLA Modules:
  0.0 39.1 jit_solution(1495111084804286602)
XLA Ops:
  0.0 0.0 copy-start.1
  0.0 2.2 %pack.1 = bf16[8,432,128]{2,1,0:T(8,128)(2,1)} custom-call(bf16[2,48,2048]{2,1,0:T(8,128)(2,1)} %image_hbm.1, bf16[2,48,2048]{2,1,0:T(8,128)(2,1)} %variance_hbm.1), custom_call_target="tpu_custom_call" | custom-call | flops 2000000000 | bytes 6000000 | tf_op jit(solution)/shard_map/pack/pallas_call | solution.py:379
  2.2 17.6 %all_to_all.5.got_ref = bf16[8,432,128]{2,1,0:T(8,128)(2,1)S(1)} all-to-all(bf16[8,432,128]{2,1,0:T(8,128)(2,1)} %pack.1), channel_id=1, replica_groups=mesh['epoch'=8,'sky'=32] {'epoch'}, dimensions={0} | all-to-all | bytes 1769472 | tf_op jit(solution)/shard_map/all_to_all | solution.py:396
  19.8 0.2 far.1
  20.0 0.0 copy-start
  20.1 0.0 copy-start.2
  20.1 6.7 %collective-permute-start = (bf16[1280,128]{1,0:T(8,128)(2,1)S(1)}, bf16[1280,128]{1,0:T(8,128)(2,1)S(1)}, u32[]{:S(2)}, u32[]{:S(2)}) collective-permute-start(bf16[1280,128]{1,0:T(8,128)(2,1)S(1)} %far.1), channel_id=1, source_target_pairs={{1,2},{2,1},{3,4},{4,3},{5,6},{6,5},{7,8},{8,7},{9,10},{10,9},{11,... | collective-permute-start | bytes 983048 | tf_op jit(solution)/shard_map/ppermute | solution.py:400
  26.8 0.2 near.1
  27.0 0.1 collective-permute-start.1
  27.1 0.0 copy-done.1
  27.1 2.0 %own.1 = (f32[16,4,48,128]{3,2,1,0:T(8,128)S(1)}, bf16[4,384,256]{2,1,0:T(8,128)(2,1)S(1)}) custom-call(f32[9]{0:T(128)S(1)} %copy-done.1, bf16[8,432,128]{2,1,0:T(8,128)(2,1)S(1)} %all_to_all.5.got_ref), custom_call_target="tpu_custom_call" | custom-call | flops 5000000000 | bytes 15000000 | tf_op jit(solution)/shard_map/own/pallas_call | solution.py:401
  29.1 0.0 collective-permute-done.1.near_ref
  29.1 0.0 copy-done
  29.2 0.0 copy-done.2
  29.2 4.0 %inner.1.stacks_in = f32[40,4,128,128]{3,2,1,0:T(8,128)S(1)} custom-call(f32[9]{0:T(128)S(1)} %copy-done.2, s32[4,16]{1,0:T(4,128)S(1)} %copy-done, f32[16,4,48,128]{3,2,1,0:T(8,128)S(1)} %get-tuple-element.8.own_ref, bf16[4,384,256]{2,1,0:T(8,128)(2,1)S(1)} %get-tuple-element.9.taps_ref, bf16[1280,128]{1,0:T(8,128)(2,1)S(1)} %collective-permute-done.1.near_ref), custom_call_target="tpu_custom_call" | custom-call | flops 5000000000 | bytes 15000000 | tf_op jit(solution)/shard_map/inner/pallas_call | solution.py:422
  33.2 1.8 %collective-permute-done.far_ref = bf16[1280,128]{1,0:T(8,128)(2,1)S(1)} collective-permute-done((bf16[1280,128]{1,0:T(8,128)(2,1)S(1)}, bf16[1280,128]{1,0:T(8,128)(2,1)S(1)}, u32[]{:S(2)}, u32[]{:S(2)}) %collective-permute-start) | collective-permute-done | bytes 327712 | tf_op jit(solution)/shard_map/ppermute | solution.py:400
  35.0 4.0 %outer.1 = (f32[48,256]{1,0:T(8,128)}, f32[40,4,128,128]{3,2,1,0:T(8,128)S(1)}) custom-call(f32[9]{0:T(128)S(1)} %copy-done.2, s32[4,16]{1,0:T(4,128)S(1)} %copy-done, f32[16,4,48,128]{3,2,1,0:T(8,128)S(1)} %get-tuple-element.8.own_ref, bf16[4,384,256]{2,1,0:T(8,128)(2,1)S(1)} %get-tuple-element.9.taps_ref, ...), custom_call_target="tpu_custom_call", output_to_operand_aliasing={{1}: (5, {})} | custom-call | flops 5000000000 | bytes 15000000 | tf_op jit(solution)/shard_map/outer/pallas_call | solution.py:432
Async XLA Ops:
  0.0 27.1 %copy-start.1 = (f32[9]{0:T(128)S(1)}, f32[9]{0:T(128)}, u32[]{:S(2)}) copy-start(f32[9]{0:T(128)} %cols_ref.1) | copy-start | bytes 112
  20.0 9.1 %copy-start = (s32[4,16]{1,0:T(4,128)S(1)}, s32[4,16]{1,0:T(4,128)}, u32[]{:S(2)}) copy-start(s32[4,16]{1,0:T(4,128)} %shift_ref.3) | copy-start | bytes 772
  20.1 9.1 %copy-start.2 = (f32[9]{0:T(128)S(1)}, f32[9]{0:T(128)}, u32[]{:S(2)}) copy-start(f32[9]{0:T(128)} %rows_ref.3) | copy-start | bytes 112
  20.1 14.9 %collective-permute-start = (bf16[1280,128]{1,0:T(8,128)(2,1)S(1)}, bf16[1280,128]{1,0:T(8,128)(2,1)S(1)}, u32[]{:S(2)}, u32[]{:S(2)}) collective-permute-start(bf16[1280,128]{1,0:T(8,128)(2,1)S(1)} %far.1), channel_id=1, source_target_pairs={{1,2},{2,1},{3,4},{4,3},{5,6},{6,5},{7,8},{8,7},{9,10},{10,9},{11,... | collective-permute-start | bytes 983048 | tf_op jit(solution)/shard_map/ppermute | solution.py:400
  27.0 2.2 %collective-permute-start.1 = (bf16[1280,128]{1,0:T(8,128)(2,1)S(1)}, bf16[1280,128]{1,0:T(8,128)(2,1)S(1)}, u32[]{:S(2)}, u32[]{:S(2)}) collective-permute-start(bf16[1280,128]{1,0:T(8,128)(2,1)S(1)} %near.1), channel_id=1, source_target_pairs={{0,1},{1,0},{2,3},{3,2},{4,5},{5,4},{6,7},{7,6},{8,9},{9,8},{10,11... | collective-permute-start | bytes 983048 | tf_op jit(solution)/shard_map/ppermute | solution.py:398

commit v3 on v2

--- a/solution.py
+++ b/solution.py
@@ -16,7 +16,8 @@
 LANES = 128
 COLS = 256
 EDGE_ROW = 8 * ROWS
-SEND_ROWS = 9 * ROWS
+PIECE = 16
+SEND_ROWS = EDGE_ROW + PIECE
 HALO = [2 * j + REACH for j in range(EPOCHS)]
 HALO_AT = [sum(HALO[:j]) for j in range(EPOCHS)]
 HALO_ROWS = sum(HALO)
@@ -36,7 +37,6 @@
 
 
 def pack_kernel(image_hbm, variance_hbm, out_hbm, held, blocks, sums, edges, arrived, sent):
-    turn = 32 * (lax.axis_index("epoch") % 4)
     lane = lax.broadcasted_iota(jnp.int32, (ROWS, LANES), 1)
     copies = []
     for a, ref in enumerate((image_hbm, variance_hbm)):
@@ -74,37 +74,49 @@
             if b < 3:
                 sums[c] = total
             else:
-                edges[c] = pltpu.roll(total, turn, 1).astype(BF16)
-    send(edges, 4, EDGE_ROW, ROWS)
+                pieces = total[:PIECE]
+                for g in range(1, ROWS // PIECE):
+                    pieces = pieces + pltpu.roll(total[g * PIECE : (g + 1) * PIECE], 32 * g, 1)
+                edges[c] = pieces.astype(BF16)
+    send(edges, 4, EDGE_ROW, PIECE)
     for copy in out:
         copy.wait()
 
 
-def build_halo(to_far, got_ref, out_ref, wide, out):
+def gather_edges(got_ref, edges_ref):
+    owner = lax.broadcasted_iota(jnp.int32, (PIECE, LANES), 1) // 32
+    pieces = [got_ref[k, EDGE_ROW:SEND_ROWS, :].astype(F32) for k in range(PEERS)]
+    for half in range(2):
+        for g in range(ROWS // PIECE):
+            total = jnp.zeros((PIECE, LANES), F32)
+            for k in range(4):
+                turn = 32 * ((k - g) % 4)
+                piece = pieces[4 * half + k]
+                total = jnp.where(owner == k, pltpu.roll(piece, turn, 1) if turn else piece, total)
+            edges_ref[half * ROWS + g * PIECE : half * ROWS + (g + 1) * PIECE, :] = total
+
+
+def build_halo(to_far, got_ref, edges_ref, out_ref, wide, out):
     core = lax.axis_index("sky") % 2
     last = core if to_far else 1 - core
-
-    def take(index, source_row, target_row, height):
-        start = source_row + last * (ROWS - height)
-        out[target_row : target_row + height, :] = wide[index, pl.ds(start, height), :]
-
     for k in range(PEERS):
         wide[k] = got_ref[k, :EDGE_ROW, :].astype(F32)
-    for half in range(2):
-        total = got_ref[4 * half, EDGE_ROW:SEND_ROWS, :].astype(F32)
-        for k in range(4 * half + 1, 4 * half + 4):
-            total = total + got_ref[k, EDGE_ROW:SEND_ROWS, :].astype(F32)
-        wide[PEERS, half * ROWS : (half + 1) * ROWS, :] = total
     for j in range(EPOCHS):
         for a in range(2):
             for t in range(2):
-                row = ((a * 2 + j % 2) * 2 + t) * ROWS
-                take(j // 2, row, (a * 2 + t) * HALO_ROWS + HALO_AT[j], HALO[j])
-    take(PEERS, 0, EDGE_LO_AT, EDGE_LO)
-    take(PEERS, ROWS, EDGE_HI_AT, EDGE_HI)
+                source = ((a * 2 + j % 2) * 2 + t) * ROWS + last * (ROWS - HALO[j])
+                row = (a * 2 + t) * HALO_ROWS + HALO_AT[j]
+                out[row : row + HALO[j], :] = wide[j // 2, pl.ds(source, HALO[j]), :]
+    out[EDGE_LO_AT:EDGE_HI_AT, :] = edges_ref[pl.ds(last * (ROWS - EDGE_LO), EDGE_LO), :]
     rest = EDGE_HI_AT + EDGE_HI
+    out[EDGE_HI_AT:rest, :] = edges_ref[pl.ds(ROWS + last * (ROWS - EDGE_HI), EDGE_HI), :]
     out[rest:HALO_SEND, :] = jnp.zeros((HALO_SEND - rest, LANES), F32)
     out_ref[...] = out[...].astype(BF16)
+
+
+def halo_kernel(to_far, got_ref, out_ref, edges_ref, wide, out):
+    gather_edges(got_ref, edges_ref)
+    build_halo(to_far, got_ref, edges_ref, out_ref, wide, out)
 
 
 def split(values):
@@ -113,8 +125,7 @@
 
 
 def column_filter(image, variance, taps):
-    high, low = split(image * variance)
-    variance = variance.astype(BF16)
+    high, low = split(image.astype(F32) * variance.astype(F32))
 
     def dot(left, right):
         return jnp.dot(left, right, preferred_element_type=F32)
@@ -124,7 +135,7 @@
     return psi, phi
 
 
-def own_kernel(cols_ref, got_ref, out_ref, taps_ref, image, variance):
+def own_kernel(cols_ref, got_ref, edges_ref, out_ref, taps_ref, image, variance):
     shape = (COLS + LANES, COLS)
     place = lax.broadcasted_iota(jnp.int32, shape, 0)
     place = jnp.where(place < COLS + LANES // 2, place, place - (COLS + LANES))
@@ -137,12 +148,6 @@
         phi_taps = jnp.where(hit, cols_ref[b] * cols_ref[b], phi_taps)
     taps_ref[0], taps_ref[1] = split(psi_taps)
     taps_ref[2], taps_ref[3] = split(phi_taps)
-    edges = []
-    for half in range(2):
-        total = got_ref[4 * half, EDGE_ROW:SEND_ROWS, :].astype(F32)
-        for k in range(4 * half + 1, 4 * half + 4):
-            total = total + got_ref[k, EDGE_ROW:SEND_ROWS, :].astype(F32)
-        edges.append(total)
     for j in range(EPOCHS):
         for a, ref in enumerate((image, variance)):
             for t in range(2):
@@ -151,8 +156,8 @@
                     j // 2, row : row + ROWS, :
                 ].astype(F32)
             turn = (LANES - REACH - edge_lane(a, j)) % LANES
-            ref[j * ROWS : (j + 1) * ROWS, COLS:] = pltpu.roll(edges[j // 8], turn, 1)
-    psi, phi = column_filter(image[...], variance[...], taps_ref)
+            ref[j * ROWS : (j + 1) * ROWS, COLS:] = pltpu.roll(edges_ref[j // 8 * ROWS : (j // 8 + 1) * ROWS, :], turn, 1)
+    psi, phi = column_filter(image[...].astype(BF16), variance[...].astype(BF16), taps_ref)
     for j in range(EPOCHS):
         rows = slice(j * ROWS, (j + 1) * ROWS)
         for t in range(2):
@@ -161,17 +166,22 @@
             out_ref[j, 2 + t] = phi[rows, lanes]
 
 
-def put_halo(above, wide, taps_ref, image, variance, filtered, maps):
-    for a, ref in enumerate((image, variance)):
-        for t in range(2):
-            start = (a * 2 + t) * HALO_ROWS
-            ref[:, t * LANES : (t + 1) * LANES] = wide[start : start + HALO_ROWS, :]
+def put_halo(above, halo_ref, taps_ref, edges, filtered, maps):
+    edges[0, : HALO_SEND - EDGE_LO_AT, :] = halo_ref[EDGE_LO_AT:HALO_SEND, :].astype(F32)
+    for a in range(2):
         for j in range(EPOCHS):
-            start, height = (EDGE_LO_AT, EDGE_LO) if j < 8 else (EDGE_HI_AT, EDGE_HI)
+            start, height = (0, EDGE_LO) if j < 8 else (EDGE_LO, EDGE_HI)
             start = start + above * (height - HALO[j])
             turn = (LANES - REACH - edge_lane(a, j)) % LANES
-            ref[HALO_AT[j] : HALO_AT[j] + HALO[j], COLS:] = pltpu.roll(wide[pl.ds(start, HALO[j]), :], turn, 1)
-    psi, phi = column_filter(image[...], variance[...], taps_ref)
+            piece = edges[0, pl.ds(start, HALO[j]), :]
+            edges[1 + a, HALO_AT[j] : HALO_AT[j] + HALO[j], :] = pltpu.roll(piece, turn, 1)
+
+    def extended(a):
+        left = halo_ref[2 * a * HALO_ROWS : (2 * a + 1) * HALO_ROWS, :]
+        right = halo_ref[(2 * a + 1) * HALO_ROWS : (2 * a + 2) * HALO_ROWS, :]
+        return jnp.concatenate([left, right, edges[1 + a].astype(BF16)], axis=1)
+
+    psi, phi = column_filter(extended(0), extended(1), taps_ref)
     for t in range(2):
         lanes = slice(t * LANES, (t + 1) * LANES)
         filtered[t] = psi[:, lanes]
@@ -220,17 +230,12 @@
     taps = [[rows_ref[a] for a in range(PSF)], [rows_ref[a] * rows_ref[a] for a in range(PSF)]]
     for j in range(EPOCHS):
         start, count = span_of(core, 0, 2 * j, far)
-        for m in range(2):
-
-            def one(t, carry, j=j, m=m, start=start, count=count):
-                p = 2 * m + t
-                total = taps[m][0] * maps[j, p, pl.ds(start - REACH, 8 * count), :]
-                for a in range(1, PSF):
-                    total = total + taps[m][a] * maps[j, p, pl.ds(start - REACH + a, 8 * count), :]
-                stacks[j, p, pl.ds(start, 8 * count), :] = total
-                return carry
-
-            lax.fori_loop(0, 2, one, 0)
+        for p in range(4):
+            factors = taps[p // 2]
+            total = factors[0] * maps[j, p, pl.ds(start - REACH, 8 * count), :]
+            for a in range(1, PSF):
+                total = total + factors[a] * maps[j, p, pl.ds(start - REACH + a, 8 * count), :]
+            stacks[j, p, pl.ds(start, 8 * count), :] = total
 
 
 BATCH = 12
@@ -265,11 +270,10 @@
 
 
 def inner_kernel(
-    rows_ref, shift_ref, own_ref, taps_ref, near_ref, stacks, wide, image, variance, filtered, maps
+    rows_ref, shift_ref, own_ref, taps_ref, near_ref, stacks, edges, filtered, maps
 ):
     core = lax.axis_index("sky") % 2
-    wide[...] = near_ref[...].astype(F32)
-    put_halo(core, wide, taps_ref, image, variance, filtered, maps)
+    put_halo(core, near_ref, taps_ref, edges, filtered, maps)
     for j in range(EPOCHS):
         for p in range(4):
             maps[j, p, BASE : BASE + ROWS, :] = own_ref[j, p]
@@ -287,9 +291,7 @@
     stacks_in,
     out_ref,
     stacks,
-    wide,
-    image,
-    variance,
+    edges,
     filtered,
     maps,
     values,
@@ -309,8 +311,7 @@
             for j in range(EPOCHS):
                 stacks[slot(level, j), :, BASE + ROWS :, :] = jnp.zeros((4, SPAN - BASE - ROWS, LANES), F32)
 
-    wide[...] = far_ref[...].astype(F32)
-    put_halo(1 - core, wide, taps_ref, image, variance, filtered, maps)
+    put_halo(1 - core, far_ref, taps_ref, edges, filtered, maps)
     own_rows = core * (ROWS - 8)
     for j in range(EPOCHS):
         for p in range(4):
@@ -360,13 +361,16 @@
     return pl.CostEstimate(flops=microseconds * 1_000_000_000, bytes_accessed=microseconds * 3_000_000, transcendentals=0)
 
 
-def send_halo(to_far, got, name):
+def build(to_far, got, name):
     return pl.pallas_call(
-        functools.partial(build_halo, to_far),
-        out_shape=jax.ShapeDtypeStruct((HALO_SEND, LANES), BF16),
+        functools.partial(halo_kernel, to_far),
+        out_shape=(
+            jax.ShapeDtypeStruct((HALO_SEND, LANES), BF16),
+            jax.ShapeDtypeStruct((2 * ROWS, LANES), F32),
+        ),
         in_specs=[vmem()],
-        out_specs=vmem(),
-        scratch_shapes=[pltpu.VMEM((PEERS + 1, EDGE_ROW, LANES), F32), pltpu.VMEM((HALO_SEND, LANES), F32)],
+        out_specs=(vmem(), vmem()),
+        scratch_shapes=[pltpu.VMEM((PEERS, EDGE_ROW, LANES), F32), pltpu.VMEM((HALO_SEND, LANES), F32)],
         compiler_params=limits(),
         cost_estimate=cost(1),
         name=name,
@@ -385,7 +389,7 @@
             pltpu.VMEM((4, ROWS, cols), BF16),
             pltpu.VMEM((4, PEERS, 2 * ROWS, LANES), BF16),
             pltpu.VMEM((PEERS, ROWS, LANES), F32),
-            pltpu.VMEM((PEERS, ROWS, LANES), BF16),
+            pltpu.VMEM((PEERS, PIECE, LANES), BF16),
             pltpu.SemaphoreType.DMA((4,)),
             pltpu.SemaphoreType.DMA((5,)),
         ],
@@ -394,9 +398,9 @@
         name="pack",
     )(image, inv_variance)
     got = lax.all_to_all(packed, "epoch", 0, 0, tiled=True)
-    near = send_halo(False, got, "near")
+    near, _ = build(False, got, "near")
+    far, edges = build(True, got, "far")
     near = lax.ppermute(near, "sky", [(i, i ^ 1) for i in range(sky_count)])
-    far = send_halo(True, got, "far")
     far = lax.ppermute(far, "sky", [(i, i + 1) if i % 2 else (i, i - 1) for i in range(1, sky_count - 1)])
     own, taps = pl.pallas_call(
         own_kernel,
@@ -404,18 +408,16 @@
             jax.ShapeDtypeStruct((EPOCHS, 4, ROWS, LANES), F32),
             jax.ShapeDtypeStruct((4, COLS + LANES, COLS), BF16),
         ),
-        in_specs=[smem(), vmem()],
+        in_specs=[smem(), vmem(), vmem()],
         out_specs=(vmem(), vmem()),
         scratch_shapes=[pltpu.VMEM((EPOCHS * ROWS, COLS + LANES), F32)] * 2,
         compiler_params=limits(),
         cost_estimate=cost(5),
         name="own",
-    )(psf_cols, got)
+    )(psf_cols, got, edges)
     stacks_shape = jax.ShapeDtypeStruct((SLOTS, 4, SPAN, LANES), F32)
     work = [
-        pltpu.VMEM((HALO_SEND, LANES), F32),
-        pltpu.VMEM((HALO_ROWS, COLS + LANES), F32),
-        pltpu.VMEM((HALO_ROWS, COLS + LANES), F32),
+        pltpu.VMEM((3, HALO_ROWS, LANES), F32),
         pltpu.VMEM((4, HALO_ROWS, LANES), F32),
         pltpu.VMEM((EPOCHS, 4, SPAN, LANES), F32),
     ]

time: 39.2 us -> 38.3 us (0.977)
    pallas_call x2, Pallas kernels: 0.42 us -> 1.03 us  [build(): pl.pallas_call(functools.partial(halo_kernel, to_far), out_shape=(jax.Sha...]
    pallas_call x1, Pallas kernels: 4.05 us -> 3.62 us  [on_device(): pl.pallas_call(outer_kernel, out_shape=(jax.ShapeDtypeStruct((ROWS, COLS)...]
  transfers between devices with their start and end apart: 2 -> 2, of which waited for: 1 -> 1; matrix products, arithmetic and copies ran while one was open for 0% -> 0% of each run, Pallas kernels for 16% -> 18%
where the time goes in v3:
time: 38.3 us; the launch traced here: 38.1 us
  blocking collectives  17.3 us (45%)
  Pallas kernels  12.7 us (33%)
  starting transfers between devices  6.61 us (17%)
  waiting for transfers between devices  1.51 us (4%)
    all_to_all x1, blocking collectives, on_device(): got = lax.all_to_all(packed, 'epoch', 0, 0, tiled=True)  17.3 us
    ppermute x1, starting transfers between devices, on_device(): lax.ppermute(far, 'sky', [(i, i + 1) if i % 2 else (i, i - 1) for i in ra...  6.61 us
    pallas_call x1, Pallas kernels, on_device(): pl.pallas_call(inner_kernel, out_shape=stacks_shape, in_specs=[smem(), sm...  3.81 us
    pallas_call x1, Pallas kernels, on_device(): pl.pallas_call(outer_kernel, out_shape=(jax.ShapeDtypeStruct((ROWS, COLS)...  3.62 us
    pallas_call x1, Pallas kernels, on_device(): pl.pallas_call(pack_kernel, out_shape=jax.ShapeDtypeStruct((PEERS, SEND_R...  2.15 us
    pallas_call x1, Pallas kernels, on_device(): pl.pallas_call(own_kernel, out_shape=(jax.ShapeDtypeStruct((EPOCHS, 4, RO...  2.07 us
    ppermute x1, waiting for transfers between devices, on_device(): lax.ppermute(far, 'sky', [(i, i + 1) if i % 2 else (i, i - 1) for i in ra...  1.51 us
    pallas_call x2, Pallas kernels, build(): pl.pallas_call(functools.partial(halo_kernel, to_far), out_shape=(jax.Sha...  1.03 us
  transfers between devices with their start and end apart: 2, of which 1 were waited for; matrix products, arithmetic and copies ran while one was open for 0% of the time, Pallas kernels for 18%

profile of v3, /device:TPU:129, one launch (start us, length us, event | category | flops | bytes accessed | tf_op | source)
XLA Modules:
  0.0 38.1 jit_solution(16421287436554015124)
XLA Ops:
  0.0 0.0 copy-start.1
  0.0 2.1 %pack.1 = bf16[8,400,128]{2,1,0:T(8,128)(2,1)} custom-call(bf16[2,48,2048]{2,1,0:T(8,128)(2,1)} %image_hbm.1, bf16[2,48,2048]{2,1,0:T(8,128)(2,1)} %variance_hbm.1), custom_call_target="tpu_custom_call" | custom-call | flops 2000000000 | bytes 6000000 | tf_op jit(solution)/shard_map/pack/pallas_call | solution.py:383
  2.2 17.3 %all_to_all.5.got_ref = bf16[8,400,128]{2,1,0:T(8,128)(2,1)S(1)} all-to-all(bf16[8,400,128]{2,1,0:T(8,128)(2,1)} %pack.1), channel_id=1, replica_groups=mesh['epoch'=8,'sky'=32] {'epoch'}, dimensions={0} | all-to-all | bytes 1638400 | tf_op jit(solution)/shard_map/all_to_all | solution.py:400
  19.4 0.2 far.1
  19.6 0.0 copy-start
  19.6 0.0 copy-start.2
  19.7 6.6 %collective-permute-start = (bf16[1280,128]{1,0:T(8,128)(2,1)S(1)}, bf16[1280,128]{1,0:T(8,128)(2,1)S(1)}, u32[]{:S(2)}, u32[]{:S(2)}) collective-permute-start(bf16[1280,128]{1,0:T(8,128)(2,1)S(1)} %get-tuple-element.14), channel_id=1, source_target_pairs={{1,2},{2,1},{3,4},{4,3},{5,6},{6,5},{7,8},{8,7},{9,10},{10,9},{11,... | collective-permute-start | bytes 983048 | tf_op jit(solution)/shard_map/ppermute | solution.py:404
  26.3 0.8 %near.1 = (bf16[1280,128]{1,0:T(8,128)(2,1)S(1)}, f32[96,128]{1,0:T(8,128)}) custom-call(bf16[8,400,128]{2,1,0:T(8,128)(2,1)S(1)} %all_to_all.5.got_ref), custom_call_target="tpu_custom_call" | custom-call | flops 1000000000 | bytes 3000000 | tf_op jit(solution)/shard_map/near/pallas_call | solution.py:365
  27.1 0.0 collective-permute-start.1
  27.1 0.0 copy-done.1
  27.1 2.1 %own.1 = (f32[16,4,48,128]{3,2,1,0:T(8,128)S(1)}, bf16[4,384,256]{2,1,0:T(8,128)(2,1)S(1)}) custom-call(f32[9]{0:T(128)S(1)} %copy-done.1, bf16[8,400,128]{2,1,0:T(8,128)(2,1)S(1)} %all_to_all.5.got_ref, f32[96,128]{1,0:T(8,128)S(1)} %get-tuple-element.11.edges_ref), custom_call_target="tpu_custom_call" | custom-call | flops 5000000000 | bytes 15000000 | tf_op jit(solution)/shard_map/own/pallas_call | solution.py:405
  29.2 0.0 collective-permute-done.1.near_ref
  29.2 0.0 copy-done
  29.2 0.0 copy-done.2
  29.2 3.8 %inner.1.stacks_in = f32[40,4,128,128]{3,2,1,0:T(8,128)S(1)} custom-call(f32[9]{0:T(128)S(1)} %copy-done.2, s32[4,16]{1,0:T(4,128)S(1)} %copy-done, f32[16,4,48,128]{3,2,1,0:T(8,128)S(1)} %get-tuple-element.12.own_ref, bf16[4,384,256]{2,1,0:T(8,128)(2,1)S(1)} %get-tuple-element.13.taps_ref, bf16[1280,128]{1,0:T(8,128)(2,1)S(1)} %collective-permute-done.1.near_ref), custom_call_target="tpu_custom_call" | custom-call | flops 5000000000 | bytes 15000000 | tf_op jit(solution)/shard_map/inner/pallas_call | solution.py:424
  33.0 1.5 %collective-permute-done.far_ref = bf16[1280,128]{1,0:T(8,128)(2,1)S(1)} collective-permute-done((bf16[1280,128]{1,0:T(8,128)(2,1)S(1)}, bf16[1280,128]{1,0:T(8,128)(2,1)S(1)}, u32[]{:S(2)}, u32[]{:S(2)}) %collective-permute-start) | collective-permute-done | bytes 327712 | tf_op jit(solution)/shard_map/ppermute | solution.py:404
  34.5 3.6 %outer.1 = (f32[48,256]{1,0:T(8,128)}, f32[40,4,128,128]{3,2,1,0:T(8,128)S(1)}) custom-call(f32[9]{0:T(128)S(1)} %copy-done.2, s32[4,16]{1,0:T(4,128)S(1)} %copy-done, f32[16,4,48,128]{3,2,1,0:T(8,128)S(1)} %get-tuple-element.12.own_ref, bf16[4,384,256]{2,1,0:T(8,128)(2,1)S(1)} %get-tuple-element.13.taps_ref, ...), custom_call_target="tpu_custom_call", output_to_operand_aliasing={{1}: (5, {})} | custom-call | flops 5000000000 | bytes 15000000 | tf_op jit(solution)/shard_map/outer/pallas_call | solution.py:434
Async XLA Ops:
  0.0 27.1 %copy-start.1 = (f32[9]{0:T(128)S(1)}, f32[9]{0:T(128)}, u32[]{:S(2)}) copy-start(f32[9]{0:T(128)} %cols_ref.1) | copy-start | bytes 112
  19.6 9.5 %copy-start = (s32[4,16]{1,0:T(4,128)S(1)}, s32[4,16]{1,0:T(4,128)}, u32[]{:S(2)}) copy-start(s32[4,16]{1,0:T(4,128)} %shift_ref.3) | copy-start | bytes 772
  19.6 9.5 %copy-start.2 = (f32[9]{0:T(128)S(1)}, f32[9]{0:T(128)}, u32[]{:S(2)}) copy-start(f32[9]{0:T(128)} %rows_ref.3) | copy-start | bytes 112
  19.7 14.9 %collective-permute-start = (bf16[1280,128]{1,0:T(8,128)(2,1)S(1)}, bf16[1280,128]{1,0:T(8,128)(2,1)S(1)}, u32[]{:S(2)}, u32[]{:S(2)}) collective-permute-start(bf16[1280,128]{1,0:T(8,128)(2,1)S(1)} %get-tuple-element.14), channel_id=1, source_target_pairs={{1,2},{2,1},{3,4},{4,3},{5,6},{6,5},{7,8},{8,7},{9,10},{10,9},{11,... | collective-permute-start | bytes 983048 | tf_op jit(solution)/shard_map/ppermute | solution.py:404
  27.1 2.1 %collective-permute-start.1 = (bf16[1280,128]{1,0:T(8,128)(2,1)S(1)}, bf16[1280,128]{1,0:T(8,128)(2,1)S(1)}, u32[]{:S(2)}, u32[]{:S(2)}) collective-permute-start(bf16[1280,128]{1,0:T(8,128)(2,1)S(1)} %get-tuple-element.15), channel_id=1, source_target_pairs={{0,1},{1,0},{2,3},{3,2},{4,5},{5,4},{6,7},{7,6},{8,9},{9,8},{10,11... | collective-permute-start | bytes 983048 | tf_op jit(solution)/shard_map/ppermute | solution.py:403

commit v4 on v3

--- a/solution.py
+++ b/solution.py
@@ -124,40 +124,78 @@
     return high, (values - high.astype(F32)).astype(BF16)
 
 
-def column_filter(image, variance, taps):
+def column_filter(image, variance, image_edge, variance_edge, taps_ref, edge_taps_ref):
     high, low = split(image.astype(F32) * variance.astype(F32))
+    edge = image_edge * variance_edge
+    edge_high = edge.astype(BF16).astype(F32)
+    lane = lax.broadcasted_iota(jnp.int32, edge.shape, 1)
+    second = (lane >= REACH) & (lane < REACH + 8)
+    third = (lane >= REACH + 8) & (lane < REACH + 16)
+    psi_edge = jnp.where(second, pltpu.roll(edge - edge_high, 8, 1), edge_high)
+    psi_edge = jnp.where(third, pltpu.roll(edge_high, 16, 1), psi_edge)
+    phi_edge = jnp.where(second, pltpu.roll(variance_edge, 8, 1), variance_edge)
 
     def dot(left, right):
         return jnp.dot(left, right, preferred_element_type=F32)
 
-    psi = dot(high, taps[0]) + (dot(low, taps[0]) + dot(high, taps[1]))
-    phi = dot(variance, taps[2]) + dot(variance, taps[3])
+    psi = dot(high, taps_ref[0]) + (dot(low, taps_ref[0]) + dot(high, taps_ref[1]))
+    psi = psi + dot(psi_edge.astype(BF16), edge_taps_ref[0])
+    phi = dot(variance, taps_ref[2]) + dot(variance, taps_ref[3])
+    phi = phi + dot(phi_edge.astype(BF16), edge_taps_ref[1])
     return psi, phi
 
 
-def own_kernel(cols_ref, got_ref, edges_ref, out_ref, taps_ref, image, variance):
-    shape = (COLS + LANES, COLS)
-    place = lax.broadcasted_iota(jnp.int32, shape, 0)
-    place = jnp.where(place < COLS + LANES // 2, place, place - (COLS + LANES))
-    step = place - lax.broadcasted_iota(jnp.int32, shape, 1) + REACH
-    psi_taps = jnp.zeros(shape, F32)
-    phi_taps = jnp.zeros(shape, F32)
+def own_kernel(
+    cols_ref, got_ref, edges_ref, out_ref, taps_ref, edge_taps_ref, image, variance, image_edge, variance_edge
+):
+    def terms(height, offset):
+        step = lax.broadcasted_iota(jnp.int32, (height, LANES), 0) - lax.broadcasted_iota(
+            jnp.int32, (height, LANES), 1
+        )
+        step = step + (offset + REACH)
+        psi_taps = jnp.zeros((height, LANES), F32)
+        phi_taps = jnp.zeros((height, LANES), F32)
+        for b in range(PSF):
+            hit = step == b
+            psi_taps = jnp.where(hit, cols_ref[b], psi_taps)
+            phi_taps = jnp.where(hit, cols_ref[b] * cols_ref[b], phi_taps)
+        return split(psi_taps) + split(phi_taps)
+
+    taps_ref[...] = jnp.zeros(taps_ref.shape, BF16)
+    for n, (on, left, right) in enumerate(zip(terms(LANES, 0), terms(16, LANES), terms(16, -16))):
+        taps_ref[n, :LANES, :LANES] = on
+        taps_ref[n, LANES:, LANES:] = on
+        taps_ref[n, LANES : LANES + 16, :LANES] = left
+        taps_ref[n, LANES - 16 : LANES, LANES:] = right
+    place = lax.broadcasted_iota(jnp.int32, (LANES, COLS), 0)
+    place = (place + REACH) % LANES
+    part, place = place // 8, place % 8
+    source = jnp.where(place < REACH, place - REACH, COLS + place - REACH)
+    step = source - lax.broadcasted_iota(jnp.int32, (LANES, COLS), 1) + REACH
+    psi_taps = jnp.zeros((LANES, COLS), F32)
+    phi_taps = jnp.zeros((LANES, COLS), F32)
     for b in range(PSF):
         hit = step == b
         psi_taps = jnp.where(hit, cols_ref[b], psi_taps)
         phi_taps = jnp.where(hit, cols_ref[b] * cols_ref[b], phi_taps)
-    taps_ref[0], taps_ref[1] = split(psi_taps)
-    taps_ref[2], taps_ref[3] = split(phi_taps)
-    for j in range(EPOCHS):
-        for a, ref in enumerate((image, variance)):
+    zero = jnp.zeros((LANES, COLS), F32)
+    psi_high = psi_taps.astype(BF16).astype(F32)
+    phi_high = phi_taps.astype(BF16).astype(F32)
+    psi_taps = jnp.where(part < 2, psi_high, jnp.where(part == 2, psi_taps - psi_high, zero))
+    phi_taps = jnp.where(part == 0, phi_high, jnp.where(part == 1, phi_taps - phi_high, zero))
+    edge_taps_ref[0] = psi_taps.astype(BF16)
+    edge_taps_ref[1] = phi_taps.astype(BF16)
+    for j in range(EPOCHS):
+        rows = slice(j * ROWS, (j + 1) * ROWS)
+        for a, (ref, edge_ref) in enumerate(((image, image_edge), (variance, variance_edge))):
             for t in range(2):
                 row = ((a * 2 + j % 2) * 2 + t) * ROWS
-                ref[j * ROWS : (j + 1) * ROWS, t * LANES : (t + 1) * LANES] = got_ref[
-                    j // 2, row : row + ROWS, :
-                ].astype(F32)
+                ref[rows, t * LANES : (t + 1) * LANES] = got_ref[j // 2, row : row + ROWS, :]
             turn = (LANES - REACH - edge_lane(a, j)) % LANES
-            ref[j * ROWS : (j + 1) * ROWS, COLS:] = pltpu.roll(edges_ref[j // 8 * ROWS : (j // 8 + 1) * ROWS, :], turn, 1)
-    psi, phi = column_filter(image[...].astype(BF16), variance[...].astype(BF16), taps_ref)
+            edge_ref[rows, :] = pltpu.roll(edges_ref[j // 8 * ROWS : (j // 8 + 1) * ROWS, :], turn, 1)
+    psi, phi = column_filter(
+        image[...], variance[...], image_edge[...], variance_edge[...], taps_ref, edge_taps_ref
+    )
     for j in range(EPOCHS):
         rows = slice(j * ROWS, (j + 1) * ROWS)
         for t in range(2):
@@ -166,7 +204,7 @@
             out_ref[j, 2 + t] = phi[rows, lanes]
 
 
-def put_halo(above, halo_ref, taps_ref, edges, filtered, maps):
+def put_halo(above, halo_ref, taps_ref, edge_taps_ref, edges, filtered, maps):
     edges[0, : HALO_SEND - EDGE_LO_AT, :] = halo_ref[EDGE_LO_AT:HALO_SEND, :].astype(F32)
     for a in range(2):
         for j in range(EPOCHS):
@@ -176,12 +214,12 @@
             piece = edges[0, pl.ds(start, HALO[j]), :]
             edges[1 + a, HALO_AT[j] : HALO_AT[j] + HALO[j], :] = pltpu.roll(piece, turn, 1)
 
-    def extended(a):
+    def both(a):
         left = halo_ref[2 * a * HALO_ROWS : (2 * a + 1) * HALO_ROWS, :]
         right = halo_ref[(2 * a + 1) * HALO_ROWS : (2 * a + 2) * HALO_ROWS, :]
-        return jnp.concatenate([left, right, edges[1 + a].astype(BF16)], axis=1)
-
-    psi, phi = column_filter(extended(0), extended(1), taps_ref)
+        return jnp.concatenate([left, right], axis=1)
+
+    psi, phi = column_filter(both(0), both(1), edges[1], edges[2], taps_ref, edge_taps_ref)
     for t in range(2):
         lanes = slice(t * LANES, (t + 1) * LANES)
         filtered[t] = psi[:, lanes]
@@ -270,10 +308,10 @@
 
 
 def inner_kernel(
-    rows_ref, shift_ref, own_ref, taps_ref, near_ref, stacks, edges, filtered, maps
+    rows_ref, shift_ref, own_ref, taps_ref, edge_taps_ref, near_ref, stacks, edges, filtered, maps
 ):
     core = lax.axis_index("sky") % 2
-    put_halo(core, near_ref, taps_ref, edges, filtered, maps)
+    put_halo(core, near_ref, taps_ref, edge_taps_ref, edges, filtered, maps)
     for j in range(EPOCHS):
         for p in range(4):
             maps[j, p, BASE : BASE + ROWS, :] = own_ref[j, p]
@@ -287,6 +325,7 @@
     shift_ref,
     own_ref,
     taps_ref,
+    edge_taps_ref,
     far_ref,
     stacks_in,
     out_ref,
@@ -311,7 +350,7 @@
             for j in range(EPOCHS):
                 stacks[slot(level, j), :, BASE + ROWS :, :] = jnp.zeros((4, SPAN - BASE - ROWS, LANES), F32)
 
-    put_halo(1 - core, far_ref, taps_ref, edges, filtered, maps)
+    put_halo(1 - core, far_ref, taps_ref, edge_taps_ref, edges, filtered, maps)
     own_rows = core * (ROWS - 8)
     for j in range(EPOCHS):
         for p in range(4):
@@ -362,15 +401,15 @@
 
 
 def build(to_far, got, name):
+    halo_shape = jax.ShapeDtypeStruct((HALO_SEND, LANES), BF16)
+    edge_shape = (2 * ROWS, LANES)
+    work = [pltpu.VMEM((PEERS, EDGE_ROW, LANES), F32), pltpu.VMEM((HALO_SEND, LANES), F32)]
     return pl.pallas_call(
         functools.partial(halo_kernel, to_far),
-        out_shape=(
-            jax.ShapeDtypeStruct((HALO_SEND, LANES), BF16),
-            jax.ShapeDtypeStruct((2 * ROWS, LANES), F32),
-        ),
+        out_shape=(halo_shape, jax.ShapeDtypeStruct(edge_shape, F32)) if to_far else halo_shape,
         in_specs=[vmem()],
-        out_specs=(vmem(), vmem()),
-        scratch_shapes=[pltpu.VMEM((PEERS, EDGE_ROW, LANES), F32), pltpu.VMEM((HALO_SEND, LANES), F32)],
+        out_specs=(vmem(), vmem()) if to_far else vmem(),
+        scratch_shapes=work if to_far else [pltpu.VMEM(edge_shape, F32), *work],
         compiler_params=limits(),
         cost_estimate=cost(1),
         name=name,
@@ -398,19 +437,20 @@
         name="pack",
     )(image, inv_variance)
     got = lax.all_to_all(packed, "epoch", 0, 0, tiled=True)
-    near, _ = build(False, got, "near")
+    near = build(False, got, "near")
     far, edges = build(True, got, "far")
     near = lax.ppermute(near, "sky", [(i, i ^ 1) for i in range(sky_count)])
     far = lax.ppermute(far, "sky", [(i, i + 1) if i % 2 else (i, i - 1) for i in range(1, sky_count - 1)])
-    own, taps = pl.pallas_call(
+    own, taps, edge_taps = pl.pallas_call(
         own_kernel,
         out_shape=(
             jax.ShapeDtypeStruct((EPOCHS, 4, ROWS, LANES), F32),
-            jax.ShapeDtypeStruct((4, COLS + LANES, COLS), BF16),
+            jax.ShapeDtypeStruct((4, COLS, COLS), BF16),
+            jax.ShapeDtypeStruct((2, LANES, COLS), BF16),
         ),
         in_specs=[smem(), vmem(), vmem()],
-        out_specs=(vmem(), vmem()),
-        scratch_shapes=[pltpu.VMEM((EPOCHS * ROWS, COLS + LANES), F32)] * 2,
+        out_specs=(vmem(), vmem(), vmem()),
+        scratch_shapes=[pltpu.VMEM((EPOCHS * ROWS, COLS), BF16)] * 2 + [pltpu.VMEM((EPOCHS * ROWS, LANES), F32)] * 2,
         compiler_params=limits(),
         cost_estimate=cost(5),
         name="own",
@@ -424,24 +464,24 @@
     stacks = pl.pallas_call(
         inner_kernel,
         out_shape=stacks_shape,
-        in_specs=[smem(), smem(), vmem(), vmem(), vmem()],
+        in_specs=[smem(), smem(), vmem(), vmem(), vmem(), vmem()],
         out_specs=vmem(),
         scratch_shapes=work,
         compiler_params=limits(),
         cost_estimate=cost(5),
         name="inner",
-    )(psf_rows, shift_num, own, taps, near)
+    )(psf_rows, shift_num, own, taps, edge_taps, near)
     out, _ = pl.pallas_call(
         outer_kernel,
         out_shape=(jax.ShapeDtypeStruct((ROWS, COLS), F32), stacks_shape),
-        in_specs=[smem(), smem(), vmem(), vmem(), vmem(), vmem()],
+        in_specs=[smem(), smem(), vmem(), vmem(), vmem(), vmem(), vmem()],
         out_specs=(vmem(), vmem()),
         scratch_shapes=[*work, pltpu.VMEM((EPOCHS, ROWS, LANES), F32)],
-        input_output_aliases={5: 1},
+        input_output_aliases={6: 1},
         compiler_params=limits(),
         cost_estimate=cost(5),
         name="outer",
-    )(psf_rows, shift_num, own, taps, far, stacks)
+    )(psf_rows, shift_num, own, taps, edge_taps, far, stacks)
     return out
 
 

time: 38.3 us -> 39.3 us (1.026)
  waiting for transfers between devices: 1.51 us -> 3.25 us
  Pallas kernels: 12.7 us -> 11.8 us
    ppermute x1, starting transfers between devices: 0.01 us -> 2.28 us  [on_device(): near = lax.ppermute(near, 'sky', [(i, i ^ 1) for i in range(sky_count)])]
    ppermute x1, starting transfers between devices: 6.61 us -> 4.43 us  [on_device(): lax.ppermute(far, 'sky', [(i, i + 1) if i % 2 else (i, i - 1) for i in ra...]
    ppermute x1, waiting for transfers between devices: 1.51 us -> 3.25 us  [on_device(): lax.ppermute(far, 'sky', [(i, i + 1) if i % 2 else (i, i - 1) for i in ra...]
    pallas_call x2, Pallas kernels: 1.03 us -> 0.43 us  [build(): pl.pallas_call(functools.partial(halo_kernel, to_far), out_shape=(halo_sh...]
  transfers between devices with their start and end apart: 2 -> 2, of which waited for: 1 -> 1; matrix products, arithmetic and copies ran while one was open for 0% -> 0% of each run, Pallas kernels for 18% -> 15%
where the time goes in v4:
time: 39.3 us; the launch traced here: 39.1 us
  blocking collectives  17.3 us (44%)
  Pallas kernels  11.8 us (30%)
  starting transfers between devices  6.71 us (17%)
  waiting for transfers between devices  3.25 us (8%)
    all_to_all x1, blocking collectives, on_device(): got = lax.all_to_all(packed, 'epoch', 0, 0, tiled=True)  17.3 us
    ppermute x1, starting transfers between devices, on_device(): lax.ppermute(far, 'sky', [(i, i + 1) if i % 2 else (i, i - 1) for i in ra...  4.43 us
    pallas_call x1, Pallas kernels, on_device(): pl.pallas_call(inner_kernel, out_shape=stacks_shape, in_specs=[smem(), sm...  3.7 us
    pallas_call x1, Pallas kernels, on_device(): pl.pallas_call(outer_kernel, out_shape=(jax.ShapeDtypeStruct((ROWS, COLS)...  3.57 us
    ppermute x1, waiting for transfers between devices, on_device(): lax.ppermute(far, 'sky', [(i, i + 1) if i % 2 else (i, i - 1) for i in ra...  3.25 us
    ppermute x1, starting transfers between devices, on_device(): near = lax.ppermute(near, 'sky', [(i, i ^ 1) for i in range(sky_count)])  2.28 us
    pallas_call x1, Pallas kernels, on_device(): pl.pallas_call(pack_kernel, out_shape=jax.ShapeDtypeStruct((PEERS, SEND_R...  2.16 us
    pallas_call x1, Pallas kernels, on_device(): pl.pallas_call(own_kernel, out_shape=(jax.ShapeDtypeStruct((EPOCHS, 4, RO...  1.97 us
  transfers between devices with their start and end apart: 2, of which 1 were waited for; matrix products, arithmetic and copies ran while one was open for 0% of the time, Pallas kernels for 15%

profile of v4, /device:TPU:129, one launch (start us, length us, event | category | flops | bytes accessed | tf_op | source)
XLA Modules:
  0.0 39.1 jit_solution(10219530713585716191)
XLA Ops:
  0.0 0.0 copy-start.1
  0.0 2.2 %pack.1 = bf16[8,400,128]{2,1,0:T(8,128)(2,1)} custom-call(bf16[2,48,2048]{2,1,0:T(8,128)(2,1)} %image_hbm.1, bf16[2,48,2048]{2,1,0:T(8,128)(2,1)} %variance_hbm.1), custom_call_target="tpu_custom_call" | custom-call | flops 2000000000 | bytes 6000000 | tf_op jit(solution)/shard_map/pack/pallas_call | solution.py:422
  2.2 17.3 %all_to_all.5.got_ref = bf16[8,400,128]{2,1,0:T(8,128)(2,1)S(1)} all-to-all(bf16[8,400,128]{2,1,0:T(8,128)(2,1)} %pack.1), channel_id=1, replica_groups=mesh['epoch'=8,'sky'=32] {'epoch'}, dimensions={0} | all-to-all | bytes 1638400 | tf_op jit(solution)/shard_map/all_to_all | solution.py:439
  19.4 0.2 near.1
  19.6 0.0 copy-start
  19.7 0.0 copy-start.2
  19.7 2.3 %collective-permute-start.1 = (bf16[1280,128]{1,0:T(8,128)(2,1)S(1)}, bf16[1280,128]{1,0:T(8,128)(2,1)S(1)}, u32[]{:S(2)}, u32[]{:S(2)}) collective-permute-start(bf16[1280,128]{1,0:T(8,128)(2,1)S(1)} %near.1), channel_id=1, source_target_pairs={{0,1},{1,0},{2,3},{3,2},{4,5},{5,4},{6,7},{7,6},{8,9},{9,8},{10,11... | collective-permute-start | bytes 983048 | tf_op jit(solution)/shard_map/ppermute | solution.py:442
  21.9 0.2 far.1
  22.2 4.4 %collective-permute-start = (bf16[1280,128]{1,0:T(8,128)(2,1)S(1)}, bf16[1280,128]{1,0:T(8,128)(2,1)S(1)}, u32[]{:S(2)}, u32[]{:S(2)}) collective-permute-start(bf16[1280,128]{1,0:T(8,128)(2,1)S(1)} %get-tuple-element.15), channel_id=1, source_target_pairs={{1,2},{2,1},{3,4},{4,3},{5,6},{6,5},{7,8},{8,7},{9,10},{10,9},{11,... | collective-permute-start | bytes 983048 | tf_op jit(solution)/shard_map/ppermute | solution.py:443
  26.6 0.0 copy-done.1
  26.6 2.0 %own.1 = (f32[16,4,48,128]{3,2,1,0:T(8,128)S(1)}, bf16[4,256,256]{2,1,0:T(8,128)(2,1)S(1)}, bf16[2,128,256]{2,1,0:T(8,128)(2,1)S(1)}) custom-call(f32[9]{0:T(128)S(1)} %copy-done.1, bf16[8,400,128]{2,1,0:T(8,128)(2,1)S(1)} %all_to_all.5.got_ref, f32[96,128]{1,0:T(8,128)S(1)} %get-tuple-element.11.edges_ref), custom_call_target="tpu_custom_call" | custom-call | flops 5000000000 | bytes 15000000 | tf_op jit(solution)/shard_map/own/pallas_call | solution.py:444
  28.6 0.0 collective-permute-done.1.near_ref
  28.6 0.0 copy-done
  28.6 0.0 copy-done.2
  28.6 3.7 %inner.1.stacks_in = f32[40,4,128,128]{3,2,1,0:T(8,128)S(1)} custom-call(f32[9]{0:T(128)S(1)} %copy-done.2, s32[4,16]{1,0:T(4,128)S(1)} %copy-done, f32[16,4,48,128]{3,2,1,0:T(8,128)S(1)} %get-tuple-element.12.own_ref, bf16[4,256,256]{2,1,0:T(8,128)(2,1)S(1)} %get-tuple-element.13.taps_ref, bf16[2,128,256]{2,1,0:T(8,128)(2,1)S(1)} %get-tuple-element.14.edge_taps_ref, ...), custom_call_target="tpu_custom_call" | custom-call | flops 5000000000 | bytes 15000000 | tf_op jit(solution)/shard_map/inner/pallas_call | solution.py:464
  32.3 3.2 %collective-permute-done.far_ref = bf16[1280,128]{1,0:T(8,128)(2,1)S(1)} collective-permute-done((bf16[1280,128]{1,0:T(8,128)(2,1)S(1)}, bf16[1280,128]{1,0:T(8,128)(2,1)S(1)}, u32[]{:S(2)}, u32[]{:S(2)}) %collective-permute-start) | collective-permute-done | bytes 327712 | tf_op jit(solution)/shard_map/ppermute | solution.py:443
  35.6 3.6 %outer.1 = (f32[48,256]{1,0:T(8,128)}, f32[40,4,128,128]{3,2,1,0:T(8,128)S(1)}) custom-call(f32[9]{0:T(128)S(1)} %copy-done.2, s32[4,16]{1,0:T(4,128)S(1)} %copy-done, f32[16,4,48,128]{3,2,1,0:T(8,128)S(1)} %get-tuple-element.12.own_ref, bf16[4,256,256]{2,1,0:T(8,128)(2,1)S(1)} %get-tuple-element.13.taps_ref, ...), custom_call_target="tpu_custom_call", output_to_operand_aliasing={{1}: (6, {})} | custom-call | flops 5000000000 | bytes 15000000 | tf_op jit(solution)/shard_map/outer/pallas_call | solution.py:474
Async XLA Ops:
  0.0 26.6 %copy-start.1 = (f32[9]{0:T(128)S(1)}, f32[9]{0:T(128)}, u32[]{:S(2)}) copy-start(f32[9]{0:T(128)} %cols_ref.1) | copy-start | bytes 112
  19.6 9.0 %copy-start = (s32[4,16]{1,0:T(4,128)S(1)}, s32[4,16]{1,0:T(4,128)}, u32[]{:S(2)}) copy-start(s32[4,16]{1,0:T(4,128)} %shift_ref.3) | copy-start | bytes 772
  19.7 9.0 %copy-start.2 = (f32[9]{0:T(128)S(1)}, f32[9]{0:T(128)}, u32[]{:S(2)}) copy-start(f32[9]{0:T(128)} %rows_ref.3) | copy-start | bytes 112
  19.7 8.9 %collective-permute-start.1 = (bf16[1280,128]{1,0:T(8,128)(2,1)S(1)}, bf16[1280,128]{1,0:T(8,128)(2,1)S(1)}, u32[]{:S(2)}, u32[]{:S(2)}) collective-permute-start(bf16[1280,128]{1,0:T(8,128)(2,1)S(1)} %near.1), channel_id=1, source_target_pairs={{0,1},{1,0},{2,3},{3,2},{4,5},{5,4},{6,7},{7,6},{8,9},{9,8},{10,11... | collective-permute-start | bytes 983048 | tf_op jit(solution)/shard_map/ppermute | solution.py:442
  22.2 13.4 %collective-permute-start = (bf16[1280,128]{1,0:T(8,128)(2,1)S(1)}, bf16[1280,128]{1,0:T(8,128)(2,1)S(1)}, u32[]{:S(2)}, u32[]{:S(2)}) collective-permute-start(bf16[1280,128]{1,0:T(8,128)(2,1)S(1)} %get-tuple-element.15), channel_id=1, source_target_pairs={{1,2},{2,1},{3,4},{4,3},{5,6},{6,5},{7,8},{8,7},{9,10},{10,9},{11,... | collective-permute-start | bytes 983048 | tf_op jit(solution)/shard_map/ppermute | solution.py:443

commit v5 on v4

--- a/solution.py
+++ b/solution.py
@@ -401,15 +401,15 @@
 
 
 def build(to_far, got, name):
-    halo_shape = jax.ShapeDtypeStruct((HALO_SEND, LANES), BF16)
-    edge_shape = (2 * ROWS, LANES)
-    work = [pltpu.VMEM((PEERS, EDGE_ROW, LANES), F32), pltpu.VMEM((HALO_SEND, LANES), F32)]
     return pl.pallas_call(
         functools.partial(halo_kernel, to_far),
-        out_shape=(halo_shape, jax.ShapeDtypeStruct(edge_shape, F32)) if to_far else halo_shape,
+        out_shape=(
+            jax.ShapeDtypeStruct((HALO_SEND, LANES), BF16),
+            jax.ShapeDtypeStruct((2 * ROWS, LANES), F32),
+        ),
         in_specs=[vmem()],
-        out_specs=(vmem(), vmem()) if to_far else vmem(),
-        scratch_shapes=work if to_far else [pltpu.VMEM(edge_shape, F32), *work],
+        out_specs=(vmem(), vmem()),
+        scratch_shapes=[pltpu.VMEM((PEERS, EDGE_ROW, LANES), F32), pltpu.VMEM((HALO_SEND, LANES), F32)],
         compiler_params=limits(),
         cost_estimate=cost(1),
         name=name,
@@ -437,7 +437,7 @@
         name="pack",
     )(image, inv_variance)
     got = lax.all_to_all(packed, "epoch", 0, 0, tiled=True)
-    near = build(False, got, "near")
+    near, _ = build(False, got, "near")
     far, edges = build(True, got, "far")
     near = lax.ppermute(near, "sky", [(i, i ^ 1) for i in range(sky_count)])
     far = lax.ppermute(far, "sky", [(i, i + 1) if i % 2 else (i, i - 1) for i in range(1, sky_count - 1)])

time: 39.3 us -> 38.3 us (0.975)
  waiting for transfers between devices: 3.25 us -> 1.73 us
  Pallas kernels: 11.8 us -> 12.4 us
    ppermute x1, starting transfers between devices: 2.28 us -> 0.01 us  [on_device(): near = lax.ppermute(near, 'sky', [(i, i ^ 1) for i in range(sky_count)])]
    ppermute x1, starting transfers between devices: 4.43 us -> 6.61 us  [on_device(): lax.ppermute(far, 'sky', [(i, i + 1) if i % 2 else (i, i - 1) for i in ra...]
    ppermute x1, waiting for transfers between devices: 3.25 us -> 1.73 us  [on_device(): lax.ppermute(far, 'sky', [(i, i + 1) if i % 2 else (i, i - 1) for i in ra...]
    pallas_call x2, Pallas kernels: 0.43 us -> 1.03 us  [build(): pl.pallas_call(functools.partial(halo_kernel, to_far), out_shape=(jax.Sha...]
  transfers between devices with their start and end apart: 2 -> 2, of which waited for: 1 -> 1; matrix products, arithmetic and copies ran while one was open for 0% -> 0% of each run, Pallas kernels for 15% -> 17%
where the time goes in v5:
time: 38.3 us; the launch traced here: 38.1 us
  blocking collectives  17.3 us (45%)
  Pallas kernels  12.4 us (32%)
  starting transfers between devices  6.61 us (17%)
  waiting for transfers between devices  1.73 us (5%)
    all_to_all x1, blocking collectives, on_device(): got = lax.all_to_all(packed, 'epoch', 0, 0, tiled=True)  17.3 us
    ppermute x1, starting transfers between devices, on_device(): lax.ppermute(far, 'sky', [(i, i + 1) if i % 2 else (i, i - 1) for i in ra...  6.61 us
    pallas_call x1, Pallas kernels, on_device(): pl.pallas_call(inner_kernel, out_shape=stacks_shape, in_specs=[smem(), sm...  3.71 us
    pallas_call x1, Pallas kernels, on_device(): pl.pallas_call(outer_kernel, out_shape=(jax.ShapeDtypeStruct((ROWS, COLS)...  3.59 us
    pallas_call x1, Pallas kernels, on_device(): pl.pallas_call(pack_kernel, out_shape=jax.ShapeDtypeStruct((PEERS, SEND_R...  2.15 us
    pallas_call x1, Pallas kernels, on_device(): pl.pallas_call(own_kernel, out_shape=(jax.ShapeDtypeStruct((EPOCHS, 4, RO...  1.96 us
    ppermute x1, waiting for transfers between devices, on_device(): lax.ppermute(far, 'sky', [(i, i + 1) if i % 2 else (i, i - 1) for i in ra...  1.73 us
    pallas_call x2, Pallas kernels, build(): pl.pallas_call(functools.partial(halo_kernel, to_far), out_shape=(jax.Sha...  1.03 us
  transfers between devices with their start and end apart: 2, of which 1 were waited for; matrix products, arithmetic and copies ran while one was open for 0% of the time, Pallas kernels for 17%

profile of v5, /device:TPU:129, one launch (start us, length us, event | category | flops | bytes accessed | tf_op | source)
XLA Modules:
  0.0 38.1 jit_solution(7360800792096077208)
XLA Ops:
  0.0 0.0 copy-start.1
  0.0 2.1 %pack.1 = bf16[8,400,128]{2,1,0:T(8,128)(2,1)} custom-call(bf16[2,48,2048]{2,1,0:T(8,128)(2,1)} %image_hbm.1, bf16[2,48,2048]{2,1,0:T(8,128)(2,1)} %variance_hbm.1), custom_call_target="tpu_custom_call" | custom-call | flops 2000000000 | bytes 6000000 | tf_op jit(solution)/shard_map/pack/pallas_call | solution.py:422
  2.2 17.3 %all_to_all.5.got_ref = bf16[8,400,128]{2,1,0:T(8,128)(2,1)S(1)} all-to-all(bf16[8,400,128]{2,1,0:T(8,128)(2,1)} %pack.1), channel_id=1, replica_groups=mesh['epoch'=8,'sky'=32] {'epoch'}, dimensions={0} | all-to-all | bytes 1638400 | tf_op jit(solution)/shard_map/all_to_all | solution.py:439
  19.4 0.2 far.1
  19.6 0.0 copy-start
  19.6 0.0 copy-start.2
  19.7 6.6 %collective-permute-start = (bf16[1280,128]{1,0:T(8,128)(2,1)S(1)}, bf16[1280,128]{1,0:T(8,128)(2,1)S(1)}, u32[]{:S(2)}, u32[]{:S(2)}) collective-permute-start(bf16[1280,128]{1,0:T(8,128)(2,1)S(1)} %get-tuple-element.16), channel_id=1, source_target_pairs={{1,2},{2,1},{3,4},{4,3},{5,6},{6,5},{7,8},{8,7},{9,10},{10,9},{11,... | collective-permute-start | bytes 983048 | tf_op jit(solution)/shard_map/ppermute | solution.py:443
  26.3 0.8 %near.1 = (bf16[1280,128]{1,0:T(8,128)(2,1)S(1)}, f32[96,128]{1,0:T(8,128)}) custom-call(bf16[8,400,128]{2,1,0:T(8,128)(2,1)S(1)} %all_to_all.5.got_ref), custom_call_target="tpu_custom_call" | custom-call | flops 1000000000 | bytes 3000000 | tf_op jit(solution)/shard_map/near/pallas_call | solution.py:404
  27.1 0.0 collective-permute-start.1
  27.1 0.0 copy-done.1
  27.1 2.0 %own.1 = (f32[16,4,48,128]{3,2,1,0:T(8,128)S(1)}, bf16[4,256,256]{2,1,0:T(8,128)(2,1)S(1)}, bf16[2,128,256]{2,1,0:T(8,128)(2,1)S(1)}) custom-call(f32[9]{0:T(128)S(1)} %copy-done.1, bf16[8,400,128]{2,1,0:T(8,128)(2,1)S(1)} %all_to_all.5.got_ref, f32[96,128]{1,0:T(8,128)S(1)} %get-tuple-element.12.edges_ref), custom_call_target="tpu_custom_call" | custom-call | flops 5000000000 | bytes 15000000 | tf_op jit(solution)/shard_map/own/pallas_call | solution.py:444
  29.1 0.0 collective-permute-done.1.near_ref
  29.1 0.0 copy-done
  29.1 0.0 copy-done.2
  29.1 3.7 %inner.1.stacks_in = f32[40,4,128,128]{3,2,1,0:T(8,128)S(1)} custom-call(f32[9]{0:T(128)S(1)} %copy-done.2, s32[4,16]{1,0:T(4,128)S(1)} %copy-done, f32[16,4,48,128]{3,2,1,0:T(8,128)S(1)} %get-tuple-element.13.own_ref, bf16[4,256,256]{2,1,0:T(8,128)(2,1)S(1)} %get-tuple-element.14.taps_ref, bf16[2,128,256]{2,1,0:T(8,128)(2,1)S(1)} %get-tuple-element.15.edge_taps_ref, ...), custom_call_target="tpu_custom_call" | custom-call | flops 5000000000 | bytes 15000000 | tf_op jit(solution)/shard_map/inner/pallas_call | solution.py:464
  32.8 1.7 %collective-permute-done.far_ref = bf16[1280,128]{1,0:T(8,128)(2,1)S(1)} collective-permute-done((bf16[1280,128]{1,0:T(8,128)(2,1)S(1)}, bf16[1280,128]{1,0:T(8,128)(2,1)S(1)}, u32[]{:S(2)}, u32[]{:S(2)}) %collective-permute-start) | collective-permute-done | bytes 327712 | tf_op jit(solution)/shard_map/ppermute | solution.py:443
  34.5 3.6 %outer.1 = (f32[48,256]{1,0:T(8,128)}, f32[40,4,128,128]{3,2,1,0:T(8,128)S(1)}) custom-call(f32[9]{0:T(128)S(1)} %copy-done.2, s32[4,16]{1,0:T(4,128)S(1)} %copy-done, f32[16,4,48,128]{3,2,1,0:T(8,128)S(1)} %get-tuple-element.13.own_ref, bf16[4,256,256]{2,1,0:T(8,128)(2,1)S(1)} %get-tuple-element.14.taps_ref, ...), custom_call_target="tpu_custom_call", output_to_operand_aliasing={{1}: (6, {})} | custom-call | flops 5000000000 | bytes 15000000 | tf_op jit(solution)/shard_map/outer/pallas_call | solution.py:474
Async XLA Ops:
  0.0 27.1 %copy-start.1 = (f32[9]{0:T(128)S(1)}, f32[9]{0:T(128)}, u32[]{:S(2)}) copy-start(f32[9]{0:T(128)} %cols_ref.1) | copy-start | bytes 112
  19.6 9.4 %copy-start = (s32[4,16]{1,0:T(4,128)S(1)}, s32[4,16]{1,0:T(4,128)}, u32[]{:S(2)}) copy-start(s32[4,16]{1,0:T(4,128)} %shift_ref.3) | copy-start | bytes 772
  19.6 9.4 %copy-start.2 = (f32[9]{0:T(128)S(1)}, f32[9]{0:T(128)}, u32[]{:S(2)}) copy-start(f32[9]{0:T(128)} %rows_ref.3) | copy-start | bytes 112
  19.7 14.9 %collective-permute-start = (bf16[1280,128]{1,0:T(8,128)(2,1)S(1)}, bf16[1280,128]{1,0:T(8,128)(2,1)S(1)}, u32[]{:S(2)}, u32[]{:S(2)}) collective-permute-start(bf16[1280,128]{1,0:T(8,128)(2,1)S(1)} %get-tuple-element.16), channel_id=1, source_target_pairs={{1,2},{2,1},{3,4},{4,3},{5,6},{6,5},{7,8},{8,7},{9,10},{10,9},{11,... | collective-permute-start | bytes 983048 | tf_op jit(solution)/shard_map/ppermute | solution.py:443
  27.1 2.0 %collective-permute-start.1 = (bf16[1280,128]{1,0:T(8,128)(2,1)S(1)}, bf16[1280,128]{1,0:T(8,128)(2,1)S(1)}, u32[]{:S(2)}, u32[]{:S(2)}) collective-permute-start(bf16[1280,128]{1,0:T(8,128)(2,1)S(1)} %get-tuple-element.17), channel_id=1, source_target_pairs={{0,1},{1,0},{2,3},{3,2},{4,5},{5,4},{6,7},{7,6},{8,9},{9,8},{10,11... | collective-permute-start | bytes 983048 | tf_op jit(solution)/shard_map/ppermute | solution.py:442

commit v6 on v5

--- a/solution.py
+++ b/solution.py
@@ -307,8 +307,31 @@
     store()
 
 
+def finish(start, height, shift_ref, stacks, values, out_ref, out_row):
+    level = LEVELS - 1
+    half = 1 << level
+    rows = pl.ds(start, height)
+    all_moves = [(moves(shift_ref, level, low), moves(shift_ref, level, low + half)) for low in range(half)]
+    for t in range(2):
+        peak = None
+        for low in range(half):
+            base_at, from_at = slot(level, low), slot(level, low + half)
+            psi_base = stacks[base_at, t, rows, :]
+            phi_base = stacks[base_at, 2 + t, rows, :]
+            for side, move in enumerate(all_moves[low]):
+                psi = psi_base + shifted(stacks, from_at, t, start, height, move)
+                phi = phi_base + shifted(stacks, from_at, 2 + t, start, height, move)
+                value = psi * lax.rsqrt(phi)
+                values[low + side * half, :height, :] = value
+                peak = value if peak is None else jnp.maximum(peak, value)
+        total = jnp.exp(values[0, :height, :] - peak)
+        for v in range(1, EPOCHS):
+            total = total + jnp.exp(values[v, :height, :] - peak)
+        out_ref[pl.ds(out_row, height), t * LANES : (t + 1) * LANES] = peak + jnp.log(total)
+
+
 def inner_kernel(
-    rows_ref, shift_ref, own_ref, taps_ref, edge_taps_ref, near_ref, stacks, edges, filtered, maps
+    rows_ref, shift_ref, own_ref, taps_ref, edge_taps_ref, near_ref, stacks, ready_ref, edges, filtered, maps, values
 ):
     core = lax.axis_index("sky") % 2
     put_halo(core, near_ref, taps_ref, edge_taps_ref, edges, filtered, maps)
@@ -318,6 +341,7 @@
     filter_rows(core, False, rows_ref, maps, stacks)
     for level in range(LEVELS - 1):
         run_level(core, False, level, shift_ref, stacks)
+    finish(BASE + (1 - core) * (ROWS - 8), 8, shift_ref, stacks, values, ready_ref, 0)
 
 
 def outer_kernel(
@@ -327,6 +351,7 @@
     taps_ref,
     edge_taps_ref,
     far_ref,
+    ready_ref,
     stacks_in,
     out_ref,
     stacks,
@@ -360,25 +385,9 @@
     for level in range(LEVELS - 1):
         run_level(core, True, level, shift_ref, stacks)
         clear(level + 1)
-    level = LEVELS - 1
-    half = 1 << level
-    last_moves = [(moves(shift_ref, level, low), moves(shift_ref, level, low + half)) for low in range(half)]
-    for t in range(2):
-        peak = None
-        for low in range(half):
-            base_at, from_at = slot(level, low), slot(level, low + half)
-            psi_base = stacks[base_at, t, BASE : BASE + ROWS, :]
-            phi_base = stacks[base_at, 2 + t, BASE : BASE + ROWS, :]
-            for side, move in enumerate(last_moves[low]):
-                psi = psi_base + shifted(stacks, from_at, t, BASE, ROWS, move)
-                phi = phi_base + shifted(stacks, from_at, 2 + t, BASE, ROWS, move)
-                value = psi * lax.rsqrt(phi)
-                values[low + side * half] = value
-                peak = value if peak is None else jnp.maximum(peak, value)
-        total = jnp.exp(values[0] - peak)
-        for v in range(1, EPOCHS):
-            total = total + jnp.exp(values[v] - peak)
-        out_ref[:, t * LANES : (t + 1) * LANES] = peak + jnp.log(total)
+    finish(BASE + 8 * core, ROWS - 8, shift_ref, stacks, values, out_ref, 8 * core)
+    ready = (1 - core) * (ROWS - 8)
+    out_ref[pl.ds(ready, 8), :] = ready_ref[...]
 
 
 SLOTS = EPOCHS + 8 * (LEVELS - 1)
@@ -460,12 +469,13 @@
         pltpu.VMEM((3, HALO_ROWS, LANES), F32),
         pltpu.VMEM((4, HALO_ROWS, LANES), F32),
         pltpu.VMEM((EPOCHS, 4, SPAN, LANES), F32),
+        pltpu.VMEM((EPOCHS, ROWS, LANES), F32),
     ]
-    stacks = pl.pallas_call(
+    stacks, ready = pl.pallas_call(
         inner_kernel,
-        out_shape=stacks_shape,
+        out_shape=(stacks_shape, jax.ShapeDtypeStruct((8, COLS), F32)),
         in_specs=[smem(), smem(), vmem(), vmem(), vmem(), vmem()],
-        out_specs=vmem(),
+        out_specs=(vmem(), vmem()),
         scratch_shapes=work,
         compiler_params=limits(),
         cost_estimate=cost(5),
@@ -474,14 +484,14 @@
     out, _ = pl.pallas_call(
         outer_kernel,
         out_shape=(jax.ShapeDtypeStruct((ROWS, COLS), F32), stacks_shape),
-        in_specs=[smem(), smem(), vmem(), vmem(), vmem(), vmem(), vmem()],
+        in_specs=[smem(), smem(), vmem(), vmem(), vmem(), vmem(), vmem(), vmem()],
         out_specs=(vmem(), vmem()),
-        scratch_shapes=[*work, pltpu.VMEM((EPOCHS, ROWS, LANES), F32)],
-        input_output_aliases={6: 1},
+        scratch_shapes=work,
+        input_output_aliases={7: 1},
         compiler_params=limits(),
         cost_estimate=cost(5),
         name="outer",
-    )(psf_rows, shift_num, own, taps, edge_taps, far, stacks)
+    )(psf_rows, shift_num, own, taps, edge_taps, far, ready, stacks)
     return out
 
 

time: 38.3 us -> 38.3 us (level)
  no operation moved by 1% of the time
where the time goes in v6:
time: 38.3 us; the launch traced here: 38.1 us
  blocking collectives  17.3 us (45%)
  Pallas kernels  12.5 us (33%)
  starting transfers between devices  6.61 us (17%)
  waiting for transfers between devices  1.59 us (4%)
    all_to_all x1, blocking collectives, on_device(): got = lax.all_to_all(packed, 'epoch', 0, 0, tiled=True)  17.3 us
    ppermute x1, starting transfers between devices, on_device(): lax.ppermute(far, 'sky', [(i, i + 1) if i % 2 else (i, i - 1) for i in ra...  6.61 us
    pallas_call x1, Pallas kernels, on_device(): pl.pallas_call(inner_kernel, out_shape=(stacks_shape, jax.ShapeDtypeStruc...  3.83 us
    pallas_call x1, Pallas kernels, on_device(): pl.pallas_call(outer_kernel, out_shape=(jax.ShapeDtypeStruct((ROWS, COLS)...  3.51 us
    pallas_call x1, Pallas kernels, on_device(): pl.pallas_call(pack_kernel, out_shape=jax.ShapeDtypeStruct((PEERS, SEND_R...  2.17 us
    pallas_call x1, Pallas kernels, on_device(): pl.pallas_call(own_kernel, out_shape=(jax.ShapeDtypeStruct((EPOCHS, 4, RO...  1.98 us
    ppermute x1, waiting for transfers between devices, on_device(): lax.ppermute(far, 'sky', [(i, i + 1) if i % 2 else (i, i - 1) for i in ra...  1.59 us
    pallas_call x2, Pallas kernels, build(): pl.pallas_call(functools.partial(halo_kernel, to_far), out_shape=(jax.Sha...  1.03 us
  transfers between devices with their start and end apart: 2, of which 1 were waited for; matrix products, arithmetic and copies ran while one was open for 0% of the time, Pallas kernels for 17%

profile of v6, /device:TPU:129, one launch (start us, length us, event | category | flops | bytes accessed | tf_op | source)
XLA Modules:
  0.0 38.1 jit_solution(17427427569220128450)
XLA Ops:
  0.0 0.0 copy-start.1
  0.0 2.2 %pack.1 = bf16[8,400,128]{2,1,0:T(8,128)(2,1)} custom-call(bf16[2,48,2048]{2,1,0:T(8,128)(2,1)} %image_hbm.1, bf16[2,48,2048]{2,1,0:T(8,128)(2,1)} %variance_hbm.1), custom_call_target="tpu_custom_call" | custom-call | flops 2000000000 | bytes 6000000 | tf_op jit(solution)/shard_map/pack/pallas_call | solution.py:431
  2.2 17.3 %all_to_all.5.got_ref = bf16[8,400,128]{2,1,0:T(8,128)(2,1)S(1)} all-to-all(bf16[8,400,128]{2,1,0:T(8,128)(2,1)} %pack.1), channel_id=1, replica_groups=mesh['epoch'=8,'sky'=32] {'epoch'}, dimensions={0} | all-to-all | bytes 1638400 | tf_op jit(solution)/shard_map/all_to_all | solution.py:448
  19.4 0.2 far.1
  19.6 0.0 copy-start
  19.7 0.0 copy-start.2
  19.7 6.6 %collective-permute-start = (bf16[1280,128]{1,0:T(8,128)(2,1)S(1)}, bf16[1280,128]{1,0:T(8,128)(2,1)S(1)}, u32[]{:S(2)}, u32[]{:S(2)}) collective-permute-start(bf16[1280,128]{1,0:T(8,128)(2,1)S(1)} %get-tuple-element.18), channel_id=1, source_target_pairs={{1,2},{2,1},{3,4},{4,3},{5,6},{6,5},{7,8},{8,7},{9,10},{10,9},{11,... | collective-permute-start | bytes 983048 | tf_op jit(solution)/shard_map/ppermute | solution.py:452
  26.3 0.8 %near.1 = (bf16[1280,128]{1,0:T(8,128)(2,1)S(1)}, f32[96,128]{1,0:T(8,128)}) custom-call(bf16[8,400,128]{2,1,0:T(8,128)(2,1)S(1)} %all_to_all.5.got_ref), custom_call_target="tpu_custom_call" | custom-call | flops 1000000000 | bytes 3000000 | tf_op jit(solution)/shard_map/near/pallas_call | solution.py:413
  27.1 0.0 collective-permute-start.1
  27.1 0.0 copy-done.1
  27.1 2.0 %own.1 = (f32[16,4,48,128]{3,2,1,0:T(8,128)S(1)}, bf16[4,256,256]{2,1,0:T(8,128)(2,1)S(1)}, bf16[2,128,256]{2,1,0:T(8,128)(2,1)S(1)}) custom-call(f32[9]{0:T(128)S(1)} %copy-done.1, bf16[8,400,128]{2,1,0:T(8,128)(2,1)S(1)} %all_to_all.5.got_ref, f32[96,128]{1,0:T(8,128)S(1)} %get-tuple-element.14.edges_ref), custom_call_target="tpu_custom_call" | custom-call | flops 5000000000 | bytes 15000000 | tf_op jit(solution)/shard_map/own/pallas_call | solution.py:453
  29.1 0.0 collective-permute-done.1.near_ref
  29.1 0.0 copy-done
  29.1 0.0 copy-done.2
  29.1 3.8 %inner.1 = (f32[40,4,128,128]{3,2,1,0:T(8,128)S(1)}, f32[8,256]{1,0:T(8,128)S(1)}) custom-call(f32[9]{0:T(128)S(1)} %copy-done.2, s32[4,16]{1,0:T(4,128)S(1)} %copy-done, f32[16,4,48,128]{3,2,1,0:T(8,128)S(1)} %get-tuple-element.15.own_ref, bf16[4,256,256]{2,1,0:T(8,128)(2,1)S(1)} %get-tuple-element.16.taps_ref, ...), custom_call_target="tpu_custom_call" | custom-call | flops 5000000000 | bytes 15000000 | tf_op jit(solution)/shard_map/inner/pallas_call | solution.py:474
  32.9 1.6 %collective-permute-done.far_ref = bf16[1280,128]{1,0:T(8,128)(2,1)S(1)} collective-permute-done((bf16[1280,128]{1,0:T(8,128)(2,1)S(1)}, bf16[1280,128]{1,0:T(8,128)(2,1)S(1)}, u32[]{:S(2)}, u32[]{:S(2)}) %collective-permute-start) | collective-permute-done | bytes 327712 | tf_op jit(solution)/shard_map/ppermute | solution.py:452
  34.5 3.5 %outer.1 = (f32[48,256]{1,0:T(8,128)}, f32[40,4,128,128]{3,2,1,0:T(8,128)S(1)}) custom-call(f32[9]{0:T(128)S(1)} %copy-done.2, s32[4,16]{1,0:T(4,128)S(1)} %copy-done, f32[16,4,48,128]{3,2,1,0:T(8,128)S(1)} %get-tuple-element.15.own_ref, bf16[4,256,256]{2,1,0:T(8,128)(2,1)S(1)} %get-tuple-element.16.taps_ref, ...), custom_call_target="tpu_custom_call", output_to_operand_aliasing={{1}: (7, {})} | custom-call | flops 5000000000 | bytes 15000000 | tf_op jit(solution)/shard_map/outer/pallas_call | solution.py:484
Async XLA Ops:
  0.0 27.1 %copy-start.1 = (f32[9]{0:T(128)S(1)}, f32[9]{0:T(128)}, u32[]{:S(2)}) copy-start(f32[9]{0:T(128)} %cols_ref.1) | copy-start | bytes 112
  19.6 9.5 %copy-start = (s32[4,16]{1,0:T(4,128)S(1)}, s32[4,16]{1,0:T(4,128)}, u32[]{:S(2)}) copy-start(s32[4,16]{1,0:T(4,128)} %shift_ref.3) | copy-start | bytes 772
  19.7 9.4 %copy-start.2 = (f32[9]{0:T(128)S(1)}, f32[9]{0:T(128)}, u32[]{:S(2)}) copy-start(f32[9]{0:T(128)} %rows_ref.3) | copy-start | bytes 112
  19.7 14.9 %collective-permute-start = (bf16[1280,128]{1,0:T(8,128)(2,1)S(1)}, bf16[1280,128]{1,0:T(8,128)(2,1)S(1)}, u32[]{:S(2)}, u32[]{:S(2)}) collective-permute-start(bf16[1280,128]{1,0:T(8,128)(2,1)S(1)} %get-tuple-element.18), channel_id=1, source_target_pairs={{1,2},{2,1},{3,4},{4,3},{5,6},{6,5},{7,8},{8,7},{9,10},{10,9},{11,... | collective-permute-start | bytes 983048 | tf_op jit(solution)/shard_map/ppermute | solution.py:452
  27.1 2.0 %collective-permute-start.1 = (bf16[1280,128]{1,0:T(8,128)(2,1)S(1)}, bf16[1280,128]{1,0:T(8,128)(2,1)S(1)}, u32[]{:S(2)}, u32[]{:S(2)}) collective-permute-start(bf16[1280,128]{1,0:T(8,128)(2,1)S(1)} %get-tuple-element.19), channel_id=1, source_target_pairs={{0,1},{1,0},{2,3},{3,2},{4,5},{5,4},{6,7},{7,6},{8,9},{9,8},{10,11... | collective-permute-start | bytes 983048 | tf_op jit(solution)/shard_map/ppermute | solution.py:451
